TPU v7x, 128 devices: a whole 4x4x4 slice. The times are simulated.
128 devices in a mesh: chan: 8 (over x, core), stn: 16 (over y, z).
Axes of the slice: x: 4, y: 4, z: 4, core: 2. Of those that a mesh axis runs over, the one named last changes fastest.
Arguments:
- voltages: bfloat16 [2, 1024, 535552], P(None, ('stn', 'chan')), may hold values from -6 to 6
- fir_taps: float32 [12, 1024], replicated, may hold values from -1.75 to 1.75
- band_start: int32 [8], replicated, may hold values from 0 to 1008, as said below
- band_count: int32 [8], replicated, may hold values from 1 to 16, as said below
- subarray: int32 [512], replicated, may hold values from 0 to 3
Outputs:
- visibilities: float32 [1024, 2, 128, 1024], P('stn', None, 'chan')
Inputs may be any that keep to these rules, and one draw needn't show every extreme that they name: `band_start`: ranges of different groups may intersect; some group's range starts at channel 1024 - 16. `band_count`: one group has exactly 16 channels and another exactly 1.
All inputs are finite; a program needn't handle non-finite values.
Results may differ from a plain program's by a relative error of at most 0.0038.
Values may be sent and summed in bfloat16 or wider, within the bound.
A program may use at most 512 MiB of HBM per device.

v0:
```python
import math

import jax
import jax.numpy as jnp
from jax import lax
from jax.sharding import PartitionSpec as P

NFFT = 1024
TAPS = 12
SPECTRA = 512
CMAX = 16


def make_table(band_start, band_count):
    groups = band_start.shape[0]
    slot_ids = jnp.arange(groups * CMAX, dtype=jnp.int32)
    group_of = slot_ids // CMAX
    offset = slot_ids % CMAX
    onehot = (group_of[:, None] == jnp.arange(groups, dtype=jnp.int32)[None, :]).astype(jnp.int32)
    first_chan = jnp.sum(onehot * band_start[None, :], axis=1)
    chan_count = jnp.sum(onehot * band_count[None, :], axis=1)
    channel = first_chan + offset
    live_mask = (offset < chan_count).astype(jnp.float32)
    phase_int = jnp.arange(NFFT, dtype=jnp.int32)[None, :] * channel[:, None] % NFFT
    angles = phase_int.astype(jnp.float32) * jnp.float32(2.0 * math.pi / NFFT)
    scaling = live_mask[:, None] * jnp.float32(1.0 / math.sqrt(NFFT))
    cosine = jnp.cos(angles) * scaling
    sine_part = jnp.sin(angles) * scaling
    stacked = jnp.stack(
        [jnp.stack([cosine, sine_part], axis=1), jnp.stack([-sine_part, cosine], axis=1)], axis=1
    )
    return stacked.astype(jnp.bfloat16)


def filter_frames(volt_block, fir_taps):
    width = volt_block.shape[1]
    framed = volt_block.reshape(2, width, SPECTRA + TAPS - 1, NFFT)

    def add_tap(tap_index, summed):
        window = lax.dynamic_slice_in_dim(framed, tap_index, SPECTRA, 2)
        weights = lax.dynamic_slice_in_dim(fir_taps, tap_index, 1, 0)
        return summed + window.astype(jnp.float32) * weights

    summed = lax.fori_loop(0, TAPS, add_tap, jnp.zeros((2, width, SPECTRA, NFFT), jnp.float32))
    return summed.astype(jnp.bfloat16)


def correlate_blocks(row_data, col_data):
    rotated = jnp.stack([row_data[:, 1], -row_data[:, 0]], axis=1)
    stacked = jnp.stack([row_data, rotated], axis=0)
    return jnp.einsum("osrit,srjt->iosj", stacked, col_data, preferred_element_type=jnp.float32)


def per_device(voltages, fir_taps, band_start, band_count, subarray):
    dft_table = make_table(band_start, band_count)
    frames = filter_frames(voltages, fir_taps)
    spectra = lax.dot_general(
        dft_table, frames, (((2, 3), (0, 3)), ((), ())), preferred_element_type=jnp.float32
    ).astype(jnp.bfloat16)
    turned = lax.all_to_all(spectra, "chan", split_axis=0, concat_axis=2, tiled=True)
    stn_index = lax.axis_index("stn")
    row_block = turned.shape[2]
    correlations = correlate_blocks(turned, lax.all_gather(turned, "stn", axis=2, tiled=True))
    stations = jnp.repeat(subarray, 2)
    own_subs = lax.dynamic_slice_in_dim(stations, stn_index * row_block, row_block, 0)
    same_array = (own_subs[:, None] == stations[None, :]).astype(jnp.float32)
    return correlations * (same_array / SPECTRA)[:, None, None, :]


def solution(mesh):
    in_specs = (P(None, ("stn", "chan"), None), P(), P(), P(), P())
    out_specs = P("stn", None, "chan", None)
    return jax.shard_map(
        per_device, mesh=mesh, in_specs=in_specs, out_specs=out_specs, check_vma=False
    )
```

profile of v0, /device:TPU:0, one launch (start us, length us, event | category | flops | bytes accessed | tf_op | source)
XLA Modules:
  0.0 786.8 jit_solution(7977719925354439112)
XLA Ops:
  8.3 493.4 %while.14 = (s32[]{:T(128)}, f32[2,8,512,1024]{3,2,1,0:T(8,128)}, bf16[2,8,523,1024]{3,1,2,0:T(8,128)(2,1)}, f32[12,1024]{1,0:T(8,128)}, s32[]{:T(128)}, /*index=5*/s32[]{:T(128)}) while((s32[]{:T(128)}, f32[2,8,512,1024]{3,2,1,0:T(8,128)}, bf16[2,8,523,1024]{3,1,2,0:T(8,128)(2,1)}, f32[12,1024]{1,0:T(8,128)}, s32[]{:T(128)}, ...), condition=%wide.region_3.4_spmd.clone, body=%wide.region_2.3_spmd.clone.sunk | while | flops 33554432 | bytes 117452888 | solution.py:44
  8.3 13.8 %constant_dynamic-slice_fusion.4 = bf16[2,8,512,1024]{3,1,2,0:T(8,128)(2,1)} fusion(bf16[2,8,523,1024]{3,1,2,0:T(8,128)(2,1)} %get-tuple-element.170, s32[]{:T(128)} %get-tuple-element.162), kind=kLoop, calls=%fused_computation.2.clone.1 | loop fusion | bytes 33554436 | tf_op jit(solution)/shard_map/while/body/eval_jaxpr/dynamic_slice | solution.py:40
  22.9 19.2 %select_add_fusion.2 = f32[2,8,512,1024]{3,2,1,0:T(8,128)} fusion(f32[2,8,512,1024]{3,2,1,0:T(8,128)} %get-tuple-element.163, bf16[2,8,512,1024]{3,1,2,0:T(8,128)(2,1)} %constant_dynamic-slice_fusion.4, f32[1024]{0:T(1024)S(1)} %bitcast.49, pred[]{:T(512)S(6)} %compare.21), kind=kLoop, calls=%fused_computation.clone.1 | loop fusion | flops 33554432 | bytes 83890176 | tf_op jit(solution)/shard_map/while/body/eval_jaxpr/add | solution.py:42
  42.1 13.8 %constant_dynamic-slice_fusion.4 = bf16[2,8,512,1024]{3,1,2,0:T(8,128)(2,1)} fusion(bf16[2,8,523,1024]{3,1,2,0:T(8,128)(2,1)} %get-tuple-element.170, s32[]{:T(128)} %get-tuple-element.162), kind=kLoop, calls=%fused_computation.2.clone.1 | loop fusion | bytes 33554436 | tf_op jit(solution)/shard_map/while/body/eval_jaxpr/dynamic_slice | solution.py:40
  56.7 27.2 %select_add_fusion.2 = f32[2,8,512,1024]{3,2,1,0:T(8,128)} fusion(f32[2,8,512,1024]{3,2,1,0:T(8,128)} %get-tuple-element.163, bf16[2,8,512,1024]{3,1,2,0:T(8,128)(2,1)} %constant_dynamic-slice_fusion.4, f32[1024]{0:T(1024)S(1)} %bitcast.49, pred[]{:T(512)S(6)} %compare.21), kind=kLoop, calls=%fused_computation.clone.1 | loop fusion | flops 33554432 | bytes 83890176 | tf_op jit(solution)/shard_map/while/body/eval_jaxpr/add | solution.py:42
  98.5 27.2 %select_add_fusion.2 = f32[2,8,512,1024]{3,2,1,0:T(8,128)} fusion(f32[2,8,512,1024]{3,2,1,0:T(8,128)} %get-tuple-element.163, bf16[2,8,512,1024]{3,1,2,0:T(8,128)(2,1)} %constant_dynamic-slice_fusion.4, f32[1024]{0:T(1024)S(1)} %bitcast.49, pred[]{:T(512)S(6)} %compare.21), kind=kLoop, calls=%fused_computation.clone.1 | loop fusion | flops 33554432 | bytes 83890176 | tf_op jit(solution)/shard_map/while/body/eval_jaxpr/add | solution.py:42
  140.3 27.2 %select_add_fusion.2 = f32[2,8,512,1024]{3,2,1,0:T(8,128)} fusion(f32[2,8,512,1024]{3,2,1,0:T(8,128)} %get-tuple-element.163, bf16[2,8,512,1024]{3,1,2,0:T(8,128)(2,1)} %constant_dynamic-slice_fusion.4, f32[1024]{0:T(1024)S(1)} %bitcast.49, pred[]{:T(512)S(6)} %compare.21), kind=kLoop, calls=%fused_computation.clone.1 | loop fusion | flops 33554432 | bytes 83890176 | tf_op jit(solution)/shard_map/while/body/eval_jaxpr/add | solution.py:42
  182.1 27.2 %select_add_fusion.2 = f32[2,8,512,1024]{3,2,1,0:T(8,128)} fusion(f32[2,8,512,1024]{3,2,1,0:T(8,128)} %get-tuple-element.163, bf16[2,8,512,1024]{3,1,2,0:T(8,128)(2,1)} %constant_dynamic-slice_fusion.4, f32[1024]{0:T(1024)S(1)} %bitcast.49, pred[]{:T(512)S(6)} %compare.21), kind=kLoop, calls=%fused_computation.clone.1 | loop fusion | flops 33554432 | bytes 83890176 | tf_op jit(solution)/shard_map/while/body/eval_jaxpr/add | solution.py:42
  223.8 27.2 %select_add_fusion.2 = f32[2,8,512,1024]{3,2,1,0:T(8,128)} fusion(f32[2,8,512,1024]{3,2,1,0:T(8,128)} %get-tuple-element.163, bf16[2,8,512,1024]{3,1,2,0:T(8,128)(2,1)} %constant_dynamic-slice_fusion.4, f32[1024]{0:T(1024)S(1)} %bitcast.49, pred[]{:T(512)S(6)} %compare.21), kind=kLoop, calls=%fused_computation.clone.1 | loop fusion | flops 33554432 | bytes 83890176 | tf_op jit(solution)/shard_map/while/body/eval_jaxpr/add | solution.py:42
  251.0 13.8 %constant_dynamic-slice_fusion.4 = bf16[2,8,512,1024]{3,1,2,0:T(8,128)(2,1)} fusion(bf16[2,8,523,1024]{3,1,2,0:T(8,128)(2,1)} %get-tuple-element.170, s32[]{:T(128)} %get-tuple-element.162), kind=kLoop, calls=%fused_computation.2.clone.1 | loop fusion | bytes 33554436 | tf_op jit(solution)/shard_map/while/body/eval_jaxpr/dynamic_slice | solution.py:40
  265.6 27.2 %select_add_fusion.2 = f32[2,8,512,1024]{3,2,1,0:T(8,128)} fusion(f32[2,8,512,1024]{3,2,1,0:T(8,128)} %get-tuple-element.163, bf16[2,8,512,1024]{3,1,2,0:T(8,128)(2,1)} %constant_dynamic-slice_fusion.4, f32[1024]{0:T(1024)S(1)} %bitcast.49, pred[]{:T(512)S(6)} %compare.21), kind=kLoop, calls=%fused_computation.clone.1 | loop fusion | flops 33554432 | bytes 83890176 | tf_op jit(solution)/shard_map/while/body/eval_jaxpr/add | solution.py:42
  292.8 13.8 %constant_dynamic-slice_fusion.4 = bf16[2,8,512,1024]{3,1,2,0:T(8,128)(2,1)} fusion(bf16[2,8,523,1024]{3,1,2,0:T(8,128)(2,1)} %get-tuple-element.170, s32[]{:T(128)} %get-tuple-element.162), kind=kLoop, calls=%fused_computation.2.clone.1 | loop fusion | bytes 33554436 | tf_op jit(solution)/shard_map/while/body/eval_jaxpr/dynamic_slice | solution.py:40
  307.4 27.2 %select_add_fusion.2 = f32[2,8,512,1024]{3,2,1,0:T(8,128)} fusion(f32[2,8,512,1024]{3,2,1,0:T(8,128)} %get-tuple-element.163, bf16[2,8,512,1024]{3,1,2,0:T(8,128)(2,1)} %constant_dynamic-slice_fusion.4, f32[1024]{0:T(1024)S(1)} %bitcast.49, pred[]{:T(512)S(6)} %compare.21), kind=kLoop, calls=%fused_computation.clone.1 | loop fusion | flops 33554432 | bytes 83890176 | tf_op jit(solution)/shard_map/while/body/eval_jaxpr/add | solution.py:42
  334.6 13.8 %constant_dynamic-slice_fusion.4 = bf16[2,8,512,1024]{3,1,2,0:T(8,128)(2,1)} fusion(bf16[2,8,523,1024]{3,1,2,0:T(8,128)(2,1)} %get-tuple-element.170, s32[]{:T(128)} %get-tuple-element.162), kind=kLoop, calls=%fused_computation.2.clone.1 | loop fusion | bytes 33554436 | tf_op jit(solution)/shard_map/while/body/eval_jaxpr/dynamic_slice | solution.py:40
  349.2 27.2 %select_add_fusion.2 = f32[2,8,512,1024]{3,2,1,0:T(8,128)} fusion(f32[2,8,512,1024]{3,2,1,0:T(8,128)} %get-tuple-element.163, bf16[2,8,512,1024]{3,1,2,0:T(8,128)(2,1)} %constant_dynamic-slice_fusion.4, f32[1024]{0:T(1024)S(1)} %bitcast.49, pred[]{:T(512)S(6)} %compare.21), kind=kLoop, calls=%fused_computation.clone.1 | loop fusion | flops 33554432 | bytes 83890176 | tf_op jit(solution)/shard_map/while/body/eval_jaxpr/add | solution.py:42
  376.4 13.8 %constant_dynamic-slice_fusion.4 = bf16[2,8,512,1024]{3,1,2,0:T(8,128)(2,1)} fusion(bf16[2,8,523,1024]{3,1,2,0:T(8,128)(2,1)} %get-tuple-element.170, s32[]{:T(128)} %get-tuple-element.162), kind=kLoop, calls=%fused_computation.2.clone.1 | loop fusion | bytes 33554436 | tf_op jit(solution)/shard_map/while/body/eval_jaxpr/dynamic_slice | solution.py:40
  390.9 27.2 %select_add_fusion.2 = f32[2,8,512,1024]{3,2,1,0:T(8,128)} fusion(f32[2,8,512,1024]{3,2,1,0:T(8,128)} %get-tuple-element.163, bf16[2,8,512,1024]{3,1,2,0:T(8,128)(2,1)} %constant_dynamic-slice_fusion.4, f32[1024]{0:T(1024)S(1)} %bitcast.49, pred[]{:T(512)S(6)} %compare.21), kind=kLoop, calls=%fused_computation.clone.1 | loop fusion | flops 33554432 | bytes 83890176 | tf_op jit(solution)/shard_map/while/body/eval_jaxpr/add | solution.py:42
  418.1 13.8 %constant_dynamic-slice_fusion.4 = bf16[2,8,512,1024]{3,1,2,0:T(8,128)(2,1)} fusion(bf16[2,8,523,1024]{3,1,2,0:T(8,128)(2,1)} %get-tuple-element.170, s32[]{:T(128)} %get-tuple-element.162), kind=kLoop, calls=%fused_computation.2.clone.1 | loop fusion | bytes 33554436 | tf_op jit(solution)/shard_map/while/body/eval_jaxpr/dynamic_slice | solution.py:40
  432.7 27.2 %select_add_fusion.2 = f32[2,8,512,1024]{3,2,1,0:T(8,128)} fusion(f32[2,8,512,1024]{3,2,1,0:T(8,128)} %get-tuple-element.163, bf16[2,8,512,1024]{3,1,2,0:T(8,128)(2,1)} %constant_dynamic-slice_fusion.4, f32[1024]{0:T(1024)S(1)} %bitcast.49, pred[]{:T(512)S(6)} %compare.21), kind=kLoop, calls=%fused_computation.clone.1 | loop fusion | flops 33554432 | bytes 83890176 | tf_op jit(solution)/shard_map/while/body/eval_jaxpr/add | solution.py:42
  459.9 13.8 %constant_dynamic-slice_fusion.4 = bf16[2,8,512,1024]{3,1,2,0:T(8,128)(2,1)} fusion(bf16[2,8,523,1024]{3,1,2,0:T(8,128)(2,1)} %get-tuple-element.170, s32[]{:T(128)} %get-tuple-element.162), kind=kLoop, calls=%fused_computation.2.clone.1 | loop fusion | bytes 33554436 | tf_op jit(solution)/shard_map/while/body/eval_jaxpr/dynamic_slice | solution.py:40
  474.5 27.2 %select_add_fusion.2 = f32[2,8,512,1024]{3,2,1,0:T(8,128)} fusion(f32[2,8,512,1024]{3,2,1,0:T(8,128)} %get-tuple-element.163, bf16[2,8,512,1024]{3,1,2,0:T(8,128)(2,1)} %constant_dynamic-slice_fusion.4, f32[1024]{0:T(1024)S(1)} %bitcast.49, pred[]{:T(512)S(6)} %compare.21), kind=kLoop, calls=%fused_computation.clone.1 | loop fusion | flops 33554432 | bytes 83890176 | tf_op jit(solution)/shard_map/while/body/eval_jaxpr/add | solution.py:42
  518.4 31.7 %all_to_all.18 = bf16[128,2,8,512]{3,2,1,0:T(8,128)(2,1)S(1)} all-to-all(bf16[128,2,8,512]{3,2,1,0:T(8,128)(2,1)S(1)} %copy.22), channel_id=1, replica_groups=mesh['chan'=8,'stn'=16] {'chan'}, dimensions={0} | all-to-all | bytes 4194304 | tf_op jit(solution)/shard_map/all_to_all | solution.py:60
  555.6 194.0 %all-gather.2.cloned.1.call-done = bf16[16,2,1024,512]{3,2,1,0:T(8,128)(2,1)} async-done(((bf16[16,2,64,512]{3,2,1,0:T(8,128)(2,1)}), bf16[16,2,1024,512]{3,2,1,0:T(8,128)(2,1)}) %all-gather.2.cloned.1.call-update) | async-done | bytes 33554448 | tf_op jit(solution)/shard_map/all_gather | solution.py:63
  749.6 18.7 %bitcast_multiply_fusion = f32[64,2,16,1024]{3,0,1,2:T(8,128)} fusion(f32[64,1024]{1,0:T(8,128)S(1)} %compare_select_fusion, bf16[1,16,2,64,512]{4,3,2,0,1:T(8,128)(2,1)} %maximum_bitcast_fusion, bf16[1,16,2,64,512]{4,3,2,0,1:T(8,128)(2,1)S(1)} %bitcast.47, bf16[16,2,1024,512]{3,2,1,0:T(8,128)(2,1)} %all-gather.2.cloned.1.call-done), kind=kOutput, calls=%fused_computation.8 | convolution fusion | flops 4305453056 | bytes 46399488 | tf_op jit(solution)/shard_map/osrit,srjt->iosj/dot_general | solution.py:51
  (43 shorter events, 100.0 us)
Async XLA Ops:
  6.5 743.1 %all-gather.2.cloned.1.call-start = ((), (), s32[]{:S(2)}) async-start(), calls=%async_computation.1 | async-start | bytes 35651584 | tf_op jit(solution)/shard_map/all_gather | solution.py:63
  8.3 493.4 %copy-start.2 = (f32[128]{0:T(128)S(1)}, f32[128]{0:T(128)}, u32[]{:S(2)}) copy-start(f32[128]{0:T(128)} %compare_select_fusion.1) | copy-start | bytes 1540
  8.3 493.4 %copy-start.3 = (s32[128]{0:T(128)S(1)}, s32[128]{0:T(128)}, u32[]{:S(2)}) copy-start(s32[128]{0:T(128)} %fusion.23) | copy-start | bytes 1540
  517.2 34.5 %copy-start.1 = (s32[512]{0:T(512)S(1)}, s32[512]{0:T(512)}, u32[]{:S(2)}) copy-start(s32[512]{0:T(512)} %param.11) | copy-start | bytes 6148
  551.7 197.9 %copy-start = (bf16[8,16,2,8,512]{4,3,0,2,1:T(8,128)(2,1)S(1)}, bf16[8,16,2,8,512]{4,3,0,2,1:T(8,128)(2,1)}, u32[]{:S(2)}) copy-start(bf16[8,16,2,8,512]{4,3,0,2,1:T(8,128)(2,1)} %copy.39) | copy-start | bytes 6291460
Sparse Core Ops, SparseCore 0:
  551.9 197.6 all-gather.1
where the time goes:
time: 790 us; the launch traced here: 787 us
  other arithmetic  326 us (41%)
  waiting for transfers between devices  194 us (25%)
  local copies, waits for them, and re-layouts  190 us (24%)
  matrix products  31.7 us (4%)
  blocking collectives  31.7 us (4%)
  between operations  13.5 us (2%)
    add x12, other arithmetic, add_tap(): return summed + window.astype(jnp.float32) * weights  318 us
    all_gather x1, waiting for transfers between devices, per_device(): lax.all_gather(turned, 'stn', axis=2, tiled=True)  194 us
    dynamic_slice x12, local copies, waits for them, and re-layouts, add_tap(): window = lax.dynamic_slice_in_dim(framed, tap_index, SPECTRA, 2)  166 us
    all_to_all x1, blocking collectives, per_device(): lax.all_to_all(spectra, 'chan', split_axis=0, concat_axis=2, tiled=True)  31.7 us
    dot_general x1, matrix products, correlate_blocks(): jnp.einsum('osrit,srjt->iosj', stacked, col_data, preferred_element_type=...  18.7 us
  transfers between devices with their start and end apart: 1, of which 1 were waited for; matrix products, arithmetic and copies ran while one was open for 0% of the time, Pallas kernels for 0%

commit v1 on v0

v1 whole, which is shorter than its diff:
```python
import math

import jax
import jax.numpy as jnp
from jax import lax
from jax.experimental import pallas as pl
from jax.experimental.pallas import tpu as pltpu
from jax.sharding import PartitionSpec as P

NFFT = 1024
TAPS = 12
SPECTRA = 512
CMAX = 16
GROUPS = 8
STEP = 128
CHUNKS = SPECTRA // STEP
f32 = jnp.float32
bf16 = jnp.bfloat16
NT = (((1,), (1,)), ((), ()))


def fill_table(start_ref, count_ref, table):
    lane = lax.broadcasted_iota(jnp.int32, (8, 128), 1)
    channel = lane % CMAX
    scale = jnp.zeros((8, 128), f32)
    for g in range(GROUPS):
        here = lane // CMAX == g
        channel = jnp.where(here, channel + start_ref[g], channel)
        live = here & (lane % CMAX < count_ref[g])
        scale = jnp.where(live, f32(1.0 / math.sqrt(NFFT)), scale)
    row = lax.broadcasted_iota(jnp.int32, (8, 128), 0)

    def rows16(k, carry):
        cosines, sines = [], []
        for half in range(2):
            phase = ((row + (k * 16 + half * 8)) * channel) & (NFFT - 1)
            angle = phase.astype(f32) * f32(2.0 * math.pi / NFFT)
            cosines.append(jnp.cos(angle) * scale)
            sines.append(jnp.sin(angle) * scale)
        cosine = jnp.concatenate(cosines, 0).astype(bf16)
        sine = jnp.concatenate(sines, 0)
        top = pl.multiple_of(k * 16, 16)
        low = pl.multiple_of(NFFT + k * 16, 16)
        table[pl.ds(top, 16), 0:128] = cosine
        table[pl.ds(top, 16), 128:256] = (-sine).astype(bf16)
        table[pl.ds(low, 16), 0:128] = sine.astype(bf16)
        table[pl.ds(low, 16), 128:256] = cosine
        return carry

    lax.fori_loop(0, NFFT // 16, rows16, 0)


def filter_chunk(volt, taps8, frames, first):
    def strip(k, carry):
        part = k // 8
        column = (k % 8) * 128
        lanes = pl.ds(pl.multiple_of(column, 128), 128)
        taps = [taps8[p, :, lanes] for p in range(TAPS)]
        window = [
            volt[part, :, pl.ds(pl.multiple_of((first + j) * NFFT + column, 128), 128)].astype(f32)
            for j in range(STEP + TAPS - 1)
        ]
        pair = []
        for u in range(STEP):
            total = window[u] * taps[0]
            for p in range(1, TAPS):
                total = total + window[u + p] * taps[p]
            pair.append(total)
            if u % 2 == 1:
                frames[part, (u - 1) * 8 : (u + 1) * 8, lanes] = jnp.concatenate(pair, 0).astype(bf16)
                pair = []
        return carry

    lax.fori_loop(0, 16, strip, 0)


def channelize_kernel(start_ref, count_ref, taps_ref, volt_hbm, out_ref, volt, taps8, table, frames, mixed, sorted_, sem):
    copies = []
    for c in range(CHUNKS):
        low = 0 if c == 0 else (c * STEP + TAPS - 1) * NFFT
        high = ((c + 1) * STEP + TAPS - 1) * NFFT
        copy = pltpu.make_async_copy(volt_hbm.at[:, :, low:high], volt.at[:, :, low:high], sem.at[c])
        copy.start()
        copies.append(copy)
    for p in range(TAPS):
        taps8[p] = jnp.broadcast_to(taps_ref[p : p + 1, :], (8, NFFT))
    fill_table(start_ref, count_ref, table)
    for c in range(CHUNKS):
        copies[c].wait()
        filter_chunk(volt, taps8, frames, c * STEP)
        product = jnp.dot(frames[0], table[0:NFFT, :], preferred_element_type=f32)
        product = product + jnp.dot(frames[1], table[NFFT:, :], preferred_element_type=f32)
        for o in range(2):
            mixed[o] = product[:, o * 128 : (o + 1) * 128]
            for i in range(8):
                sorted_[o, pl.ds(i, 128, stride=8), :] = mixed[o, pl.ds(i, STEP, stride=8), :].T
            tile = sorted_[o].reshape(GROUPS, CMAX, 8, STEP).astype(bf16)
            out_ref[:, c, :, :, o * 128 : (o + 1) * 128] = tile


def channelize(voltages, fir_taps, band_start, band_count):
    return pl.pallas_call(
        channelize_kernel,
        name="channelize",
        out_shape=jax.ShapeDtypeStruct((GROUPS, CHUNKS, CMAX, 8, 2 * STEP), bf16),
        in_specs=[pl.BlockSpec(memory_space=pltpu.SMEM)] * 2
        + [pl.BlockSpec(memory_space=pltpu.VMEM), pl.BlockSpec(memory_space=pl.ANY)],
        out_specs=pl.BlockSpec(memory_space=pltpu.VMEM),
        scratch_shapes=[
            pltpu.VMEM(voltages.shape, bf16),
            pltpu.VMEM((TAPS, 8, NFFT), f32),
            pltpu.VMEM((2 * NFFT, 256), bf16),
            pltpu.VMEM((2, STEP * 8, NFFT), bf16),
            pltpu.VMEM((2, STEP * 8, 128), f32),
            pltpu.VMEM((2, 128 * 8, 128), f32),
            pltpu.SemaphoreType.DMA((CHUNKS,)),
        ],
        compiler_params=pltpu.CompilerParams(vmem_limit_bytes=58 << 20),
    )(band_start, band_count, fir_taps, voltages)


def correlate_kernel(row_ref, all_ref, out_ref):
    total = None
    for c in range(CHUNKS):
        rows = row_ref[c]
        turned = jnp.concatenate([rows[:, STEP:], -rows[:, :STEP]], axis=1)
        both = jnp.concatenate([rows, turned], axis=0)
        part = lax.dot_general(both, all_ref[c], NT, preferred_element_type=f32)
        total = part if total is None else total + part
    out_ref[0] = total.reshape(2, row_ref.shape[1], -1).astype(bf16)


def correlate(spectra, blocks):
    inputs = spectra.shape[1]
    rows = inputs // blocks
    return pl.pallas_call(
        correlate_kernel,
        name="correlate",
        grid=(blocks,),
        out_shape=jax.ShapeDtypeStruct((blocks, 2, rows, inputs), bf16),
        in_specs=[
            pl.BlockSpec((CHUNKS, rows, 2 * STEP), lambda k: (0, k, 0)),
            pl.BlockSpec(memory_space=pltpu.VMEM),
        ],
        out_specs=pl.BlockSpec((1, 2, rows, inputs), lambda k: (k, 0, 0, 0)),
        compiler_params=pltpu.CompilerParams(vmem_limit_bytes=40 << 20),
    )(spectra, spectra)


def place_kernel(in_ref, mask_ref, out_ref, scratch):
    mask = mask_ref[...]
    for q in range(CMAX):
        for o in range(2):
            values = in_ref[q, o].astype(f32) * mask
            for part in range(8):
                for half in range(2):
                    scratch[part, pl.ds(half * 256 + o * 16 + q, 8, stride=32), :] = values[
                        half * 8 : (half + 1) * 8, part * 128 : (part + 1) * 128
                    ]
    for part in range(8):
        out_ref[:, part * 128 : (part + 1) * 128] = scratch[part]


def place(blocks, mask):
    slots, _, rows, inputs = blocks.shape
    flat = pl.pallas_call(
        place_kernel,
        name="place",
        grid=(rows // 16,),
        out_shape=jax.ShapeDtypeStruct((rows * 2 * slots, inputs), f32),
        in_specs=[
            pl.BlockSpec((slots, 2, 16, inputs), lambda b: (0, 0, b, 0)),
            pl.BlockSpec((16, inputs), lambda b: (b, 0)),
        ],
        out_specs=pl.BlockSpec((16 * 2 * slots, inputs), lambda b: (b, 0)),
        scratch_shapes=[pltpu.VMEM((8, 16 * 2 * slots, 128), f32)],
        compiler_params=pltpu.CompilerParams(vmem_limit_bytes=40 << 20),
    )(blocks, mask)
    return flat.reshape(rows, 2, slots, inputs)


def per_device(voltages, fir_taps, band_start, band_count, subarray):
    spectra = channelize(voltages, fir_taps, band_start, band_count)
    spectra = lax.all_to_all(spectra, "chan", split_axis=0, concat_axis=0, tiled=True)
    spectra = jnp.transpose(spectra, (2, 1, 0, 3, 4))
    spectra = lax.all_to_all(spectra, "stn", split_axis=0, concat_axis=0, tiled=True)
    spectra = jnp.transpose(spectra, (1, 0, 2, 3, 4)).reshape(CHUNKS, -1, 2 * STEP)
    blocks = correlate(spectra, lax.axis_size("stn"))
    blocks = lax.all_to_all(blocks, "stn", split_axis=0, concat_axis=0, tiled=True)
    rows = blocks.shape[2]
    stations = jnp.repeat(subarray, 2)
    own = lax.dynamic_slice_in_dim(stations, lax.axis_index("stn") * rows, rows, 0)
    mask = (own[:, None] == stations[None, :]).astype(f32) / SPECTRA
    return place(blocks, mask)


def solution(mesh):
    in_specs = (P(None, ("stn", "chan"), None), P(), P(), P(), P())
    out_specs = P("stn", None, "chan", None)
    return jax.shard_map(
        per_device, mesh=mesh, in_specs=in_specs, out_specs=out_specs, check_vma=False
    )
```

time: 790 us -> 198 us (0.25)
  other arithmetic: 326 us -> 0.09 us
  local copies, waits for them, and re-layouts: 190 us -> 2.92 us
  waiting for transfers between devices: 194 us -> 52.4 us
  Pallas kernels: 0 us -> 70.2 us
  blocking collectives: 31.7 us -> 67.7 us
  matrix products: 31.7 us -> 0 us
  between operations: 13.5 us -> 0.08 us
    add x13 -> x0, other arithmetic: 319 us -> none  [the longest x12 318 us: add_tap(): return summed + window.astype(jnp.float32) * weights]
    all_gather x1 -> x0, waiting for transfers between devices: 194 us -> none  [per_device(): lax.all_gather(turned, 'stn', axis=2, tiled=True)]
    dynamic_slice x25 -> x1, local copies, waits for them, and re-layouts: 175 us -> 0.08 us  [per_device(): lax.dynamic_slice_in_dim(stations, lax.axis_index('stn') * rows, rows, 0)]
    pallas_call x0 -> x3, Pallas kernels: none -> 70.2 us  [the longest x1 45.1 us: channelize(): pl.pallas_call(channelize_kernel, name='channelize', out_shape=jax.ShapeD...]
    all_to_all x0 -> x1, waiting for transfers between devices: none -> 52.4 us  [per_device(): lax.all_to_all(blocks, 'stn', split_axis=0, concat_axis=0, tiled=True)]
    all_to_all x1 -> x2, blocking collectives: 31.7 us -> 67.7 us  [the longest x1 35.8 us: per_device(): lax.all_to_all(spectra, 'stn', split_axis=0, concat_axis=0, tiled=True)]
    dot_general x2 -> x0, matrix products: 31.7 us -> none  [the longest x1 18.7 us: correlate_blocks(): jnp.einsum('osrit,srjt->iosj', stacked, col_data, preferred_element_type=...]
    mul x1 -> x0, local copies, waits for them, and re-layouts: 11.6 us -> none  [per_device(): return correlations * (same_array / SPECTRA)[:, None, None, :]]
where the time goes in v1:
time: 198 us
  Pallas kernels  70.2 us (35%)
  blocking collectives  67.7 us (34%)
  waiting for transfers between devices  52.4 us (26%)
  starting transfers between devices  4.67 us (2%)
  local copies, waits for them, and re-layouts  2.92 us (1%)
    all_to_all x1, waiting for transfers between devices, per_device(): lax.all_to_all(blocks, 'stn', split_axis=0, concat_axis=0, tiled=True)  52.4 us
    pallas_call x1, Pallas kernels, channelize(): pl.pallas_call(channelize_kernel, name='channelize', out_shape=jax.ShapeD...  45.1 us
    all_to_all x1, blocking collectives, per_device(): lax.all_to_all(spectra, 'stn', split_axis=0, concat_axis=0, tiled=True)  35.8 us
    all_to_all x1, blocking collectives, per_device(): lax.all_to_all(spectra, 'chan', split_axis=0, concat_axis=0, tiled=True)  31.9 us
    pallas_call x1, Pallas kernels, correlate(): pl.pallas_call(correlate_kernel, name='correlate', grid=(blocks,), out_sh...  13.1 us
    pallas_call x1, Pallas kernels, place(): pl.pallas_call(place_kernel, name='place', grid=(rows // 16,), out_shape=...  12 us
    all_to_all x1, starting transfers between devices, per_device(): lax.all_to_all(blocks, 'stn', split_axis=0, concat_axis=0, tiled=True)  4.67 us
  transfers between devices with their start and end apart: 1, of which 1 were waited for; matrix products, arithmetic and copies ran while one was open for 0% of the time, Pallas kernels for 0%

profile of v1, /device:TPU:0, one launch (start us, length us, event | category | flops | bytes accessed | tf_op | source)
XLA Modules:
  0.0 198.1 jit_solution(12633239628763693551)
XLA Ops:
  0.0 45.1 %channelize.1 = bf16[8,4,16,8,256]{4,3,2,1,0:T(8,128)(2,1)} custom-call(s32[8]{0:T(128)} %start_ref.1, s32[8]{0:T(128)} %count_ref.1, f32[12,1024]{1,0:T(8,128)} %taps_ref.1, bf16[2,8,535552]{2,1,0:T(8,128)(2,1)} %volt_hbm.1), custom_call_target="tpu_custom_call" | custom-call | tf_op jit(solution)/shard_map/channelize/pallas_call | solution.py:102
  45.1 31.9 %all_to_all.15 = bf16[8,4,16,8,256]{4,3,2,1,0:T(8,128)(2,1)S(1)} all-to-all(bf16[8,4,16,8,256]{4,3,2,1,0:T(8,128)(2,1)} %channelize.1), channel_id=1, replica_groups=mesh['chan'=8,'stn'=16] {'chan'}, dimensions={0} | all-to-all | bytes 4194304 | tf_op jit(solution)/shard_map/all_to_all | solution.py:184
  77.0 0.3 copy.8
  77.3 35.8 %all_to_all.16 = bf16[16,4,8,8,256]{4,3,1,2,0:T(8,128)(2,1)S(1)} all-to-all(bf16[16,4,8,8,256]{4,3,1,2,0:T(8,128)(2,1)S(1)} %copy.8), channel_id=1, replica_groups=mesh['chan'=8,'stn'=16] {'stn'}, dimensions={0} | all-to-all | bytes 4194304 | tf_op jit(solution)/shard_map/all_to_all | solution.py:186
  113.1 0.3 copy.9
  113.4 13.1 %correlate.1 = bf16[16,2,64,1024]{3,2,1,0:T(8,128)(2,1)S(1)} custom-call(bf16[4,1024,256]{2,1,0:T(8,128)(2,1)S(1)} %bitcast.4, bf16[4,1024,256]{2,1,0:T(8,128)(2,1)S(1)} %bitcast.5), custom_call_target="tpu_custom_call" | custom-call | tf_op jit(solution)/shard_map/correlate/pallas_call | solution.py:136
  126.5 0.0 copy-start
  126.5 2.0 %copy-done = bf16[16,2,64,1024]{3,2,1,0:T(8,128)(2,1)} copy-done((bf16[16,2,64,1024]{3,2,1,0:T(8,128)(2,1)}, bf16[16,2,64,1024]{3,2,1,0:T(8,128)(2,1)S(1)}, u32[]{:S(2)}) %copy-start) | copy-done | bytes 4194328
  128.5 0.0 copy-start.1
  128.5 4.7 %all-to-all-start.2 = ((bf16[16,2,64,1024]{3,2,1,0:T(8,128)(2,1)}), bf16[16,2,64,1024]{3,2,1,0:T(8,128)(2,1)}, u32[]{:S(2)}, u32[]{:S(2)}) async-start(bf16[16,2,64,1024]{3,2,1,0:T(8,128)(2,1)} %copy-done), calls=%async_computation.2 | async-start | bytes 8388608 | tf_op jit(solution)/shard_map/all_to_all | solution.py:189
  133.2 0.0 copy-done.1
  133.2 0.1 broadcast_in_dim.4
  133.3 0.2 reshape.12
  133.5 0.1 dynamic_slice.3
  133.6 0.1 compare_select_fusion.mask_ref
  133.7 52.4 %all-to-all-done.2.in_ref = bf16[16,2,64,1024]{3,2,1,0:T(8,128)(2,1)} async-done(((bf16[16,2,64,1024]{3,2,1,0:T(8,128)(2,1)}), bf16[16,2,64,1024]{3,2,1,0:T(8,128)(2,1)}, u32[]{:S(2)}, u32[]{:S(2)}) %all-to-all-start.2) | async-done | bytes 4194336 | tf_op jit(solution)/shard_map/all_to_all | solution.py:189
  186.1 12.0 %place.1 = f32[2048,1024]{1,0:T(8,128)} custom-call(bf16[16,2,64,1024]{3,2,1,0:T(8,128)(2,1)} %all-to-all-done.2.in_ref, f32[64,1024]{1,0:T(8,128)S(1)} %compare_select_fusion.mask_ref), custom_call_target="tpu_custom_call" | custom-call | tf_op jit(solution)/shard_map/place/pallas_call | solution.py:166
Async XLA Ops:
  126.5 2.0 %copy-start = (bf16[16,2,64,1024]{3,2,1,0:T(8,128)(2,1)}, bf16[16,2,64,1024]{3,2,1,0:T(8,128)(2,1)S(1)}, u32[]{:S(2)}) copy-start(bf16[16,2,64,1024]{3,2,1,0:T(8,128)(2,1)S(1)} %correlate.1) | copy-start | bytes 12582916
  128.5 4.7 %copy-start.1 = (s32[512]{0:T(512)S(1)}, s32[512]{0:T(512)}, u32[]{:S(2)}) copy-start(s32[512]{0:T(512)} %param.9) | copy-start | bytes 6148
  128.5 57.6 %all-to-all-start.2 = ((bf16[16,2,64,1024]{3,2,1,0:T(8,128)(2,1)}), bf16[16,2,64,1024]{3,2,1,0:T(8,128)(2,1)}, u32[]{:S(2)}, u32[]{:S(2)}) async-start(bf16[16,2,64,1024]{3,2,1,0:T(8,128)(2,1)} %copy-done), calls=%async_computation.2 | async-start | bytes 8388608 | tf_op jit(solution)/shard_map/all_to_all | solution.py:189

commit v2 on v1

--- a/solution.py
+++ b/solution.py
@@ -16,6 +16,7 @@
 CHUNKS = SPECTRA // STEP
 f32 = jnp.float32
 bf16 = jnp.bfloat16
+MESH = pl.DeviceIdType.MESH
 NT = (((1,), (1,)), ((), ()))
 
 
@@ -74,19 +75,71 @@
     lax.fori_loop(0, 16, strip, 0)
 
 
-def channelize_kernel(start_ref, count_ref, taps_ref, volt_hbm, out_ref, volt, taps8, table, frames, mixed, sorted_, sem):
-    copies = []
+def total_wait(ref, sem):
+    pltpu.make_async_copy(ref, ref, sem).wait()
+
+
+def correlator_kernel(
+    start_ref, count_ref, taps_ref, volt_hbm, out_ref,
+    volt, taps8, table, frames, mixed, sorted_, outgoing, passing, held, results,
+    volt_sem, send_a, recv_a, send_b, recv_b, send_c, recv_c,
+):
+    chan, stn = lax.axis_index("chan"), lax.axis_index("stn")
+    chans, stns = lax.axis_size("chan"), lax.axis_size("stn")
+
+    def volt_copy(c, first):
+        low = first * NFFT
+        wide = STEP * NFFT
+        span = pl.ds(pl.multiple_of(low, 128), wide)
+        return pltpu.make_async_copy(volt_hbm.at[:, :, span], volt.at[:, :, span], volt_sem.at[c])
+
+    halo = pl.ds(SPECTRA * NFFT, (TAPS - 1) * NFFT)
+    halo_copy = pltpu.make_async_copy(volt_hbm.at[:, :, halo], volt.at[:, :, halo], volt_sem.at[CHUNKS])
     for c in range(CHUNKS):
-        low = 0 if c == 0 else (c * STEP + TAPS - 1) * NFFT
-        high = ((c + 1) * STEP + TAPS - 1) * NFFT
-        copy = pltpu.make_async_copy(volt_hbm.at[:, :, low:high], volt.at[:, :, low:high], sem.at[c])
-        copy.start()
-        copies.append(copy)
+        volt_copy(c, c * STEP).start()
+    halo_copy.start()
+
+    barrier = pltpu.get_barrier_semaphore()
+    for d in range(1, chans):
+        pl.semaphore_signal(barrier, inc=1, device_id=((chan + d) % chans, stn), device_id_type=MESH)
+    for d in range(1, stns):
+        pl.semaphore_signal(barrier, inc=1, device_id=(chan, (stn + d) % stns), device_id_type=MESH)
+
     for p in range(TAPS):
         taps8[p] = jnp.broadcast_to(taps_ref[p : p + 1, :], (8, NFFT))
     fill_table(start_ref, count_ref, table)
-    for c in range(CHUNKS):
-        copies[c].wait()
+    pl.semaphore_wait(barrier, chans + stns - 2)
+
+    def send_chan(c):
+        for d in range(1, chans):
+            to = (chan + d) % chans
+            pltpu.make_async_remote_copy(
+                outgoing.at[c, to], passing.at[c, chan], send_a, recv_a.at[c],
+                device_id=(to, stn), device_id_type=MESH,
+            ).start()
+        pltpu.make_async_copy(outgoing.at[c, chan], passing.at[c, chan], recv_a.at[c]).start()
+
+    def send_stn(c):
+        total_wait(passing.at[c], recv_a.at[c])
+        for d in range(1, stns):
+            to = (stn + d) % stns
+            pltpu.make_async_remote_copy(
+                passing.at[c, :, to], held.at[c, stn], send_b, recv_b.at[c],
+                device_id=(chan, to), device_id_type=MESH,
+            ).start()
+        pltpu.make_async_copy(passing.at[c, :, stn], held.at[c, stn], recv_b.at[c]).start()
+
+    volt_copy(0, 0).wait()
+
+    def chunk(c, carry):
+        @pl.when(c < CHUNKS - 1)
+        def _():
+            volt_copy(c + 1, (c + 1) * STEP).wait()
+
+        @pl.when(c == CHUNKS - 1)
+        def _():
+            halo_copy.wait()
+
         filter_chunk(volt, taps8, frames, c * STEP)
         product = jnp.dot(frames[0], table[0:NFFT, :], preferred_element_type=f32)
         product = product + jnp.dot(frames[1], table[NFFT:, :], preferred_element_type=f32)
@@ -95,17 +148,67 @@
             for i in range(8):
                 sorted_[o, pl.ds(i, 128, stride=8), :] = mixed[o, pl.ds(i, STEP, stride=8), :].T
             tile = sorted_[o].reshape(GROUPS, CMAX, 8, STEP).astype(bf16)
-            out_ref[:, c, :, :, o * 128 : (o + 1) * 128] = tile
-
-
-def channelize(voltages, fir_taps, band_start, band_count):
+            outgoing[c, :, :, :, o * 128 : (o + 1) * 128] = tile
+        send_chan(c)
+
+        @pl.when(c > 0)
+        def _():
+            send_stn(c - 1)
+
+        return carry
+
+    lax.fori_loop(0, CHUNKS, chunk, 0)
+    send_stn(CHUNKS - 1)
+    for c in range(CHUNKS):
+        total_wait(held.at[c], recv_b.at[c])
+
+    inputs = stns * chans * 8
+    rows = chans * 8
+
+    def correlate(s, carry):
+        k = (stn + 7 * (s + 1)) % stns
+        total = None
+        for c in range(CHUNKS):
+            own = held[c, k].reshape(rows, 2 * STEP)
+            turned = jnp.concatenate([own[:, STEP:], -own[:, :STEP]], axis=1)
+            both = jnp.concatenate([own, turned], axis=0)
+            part = lax.dot_general(
+                both, held[c].reshape(inputs, 2 * STEP), NT, preferred_element_type=f32
+            )
+            total = part if total is None else total + part
+        results[k] = total.reshape(2, rows, inputs).astype(bf16)
+
+        @pl.when(s < stns - 1)
+        def _():
+            pltpu.make_async_remote_copy(
+                results.at[k], out_ref.at[stn], send_c, recv_c,
+                device_id=(chan, k), device_id_type=MESH,
+            ).start()
+
+        @pl.when(s == stns - 1)
+        def _():
+            pltpu.make_async_copy(results.at[k], out_ref.at[stn], recv_c).start()
+
+        return carry
+
+    lax.fori_loop(0, stns, correlate, 0)
+    total_wait(outgoing.at[:, 0 : chans - 1], send_a)
+    total_wait(held.at[:, 0 : stns - 1], send_b)
+    total_wait(results.at[0 : stns - 1], send_c)
+    total_wait(out_ref, recv_c)
+
+
+def correlator(voltages, fir_taps, band_start, band_count):
+    chans, stns = lax.axis_size("chan"), lax.axis_size("stn")
+    inputs = stns * chans * 8
+    blocks = (stns, 2, chans * 8, inputs)
     return pl.pallas_call(
-        channelize_kernel,
-        name="channelize",
-        out_shape=jax.ShapeDtypeStruct((GROUPS, CHUNKS, CMAX, 8, 2 * STEP), bf16),
+        correlator_kernel,
+        name="correlator",
+        out_shape=jax.ShapeDtypeStruct(blocks, bf16),
         in_specs=[pl.BlockSpec(memory_space=pltpu.SMEM)] * 2
         + [pl.BlockSpec(memory_space=pltpu.VMEM), pl.BlockSpec(memory_space=pl.ANY)],
-        out_specs=pl.BlockSpec(memory_space=pltpu.VMEM),
+        out_specs=pl.BlockSpec(memory_space=pl.ANY),
         scratch_shapes=[
             pltpu.VMEM(voltages.shape, bf16),
             pltpu.VMEM((TAPS, 8, NFFT), f32),
@@ -113,38 +216,22 @@
             pltpu.VMEM((2, STEP * 8, NFFT), bf16),
             pltpu.VMEM((2, STEP * 8, 128), f32),
             pltpu.VMEM((2, 128 * 8, 128), f32),
+            pltpu.VMEM((CHUNKS, chans, CMAX, 8, 2 * STEP), bf16),
+            pltpu.VMEM((CHUNKS, chans, CMAX, 8, 2 * STEP), bf16),
+            pltpu.VMEM((CHUNKS, stns, chans, 8, 2 * STEP), bf16),
+            pltpu.VMEM(blocks, bf16),
+            pltpu.SemaphoreType.DMA((CHUNKS + 1,)),
+            pltpu.SemaphoreType.DMA,
             pltpu.SemaphoreType.DMA((CHUNKS,)),
+            pltpu.SemaphoreType.DMA,
+            pltpu.SemaphoreType.DMA((CHUNKS,)),
+            pltpu.SemaphoreType.DMA,
+            pltpu.SemaphoreType.DMA,
         ],
-        compiler_params=pltpu.CompilerParams(vmem_limit_bytes=58 << 20),
+        compiler_params=pltpu.CompilerParams(
+            collective_id=0, has_side_effects=True, vmem_limit_bytes=58 << 20
+        ),
     )(band_start, band_count, fir_taps, voltages)
-
-
-def correlate_kernel(row_ref, all_ref, out_ref):
-    total = None
-    for c in range(CHUNKS):
-        rows = row_ref[c]
-        turned = jnp.concatenate([rows[:, STEP:], -rows[:, :STEP]], axis=1)
-        both = jnp.concatenate([rows, turned], axis=0)
-        part = lax.dot_general(both, all_ref[c], NT, preferred_element_type=f32)
-        total = part if total is None else total + part
-    out_ref[0] = total.reshape(2, row_ref.shape[1], -1).astype(bf16)
-
-
-def correlate(spectra, blocks):
-    inputs = spectra.shape[1]
-    rows = inputs // blocks
-    return pl.pallas_call(
-        correlate_kernel,
-        name="correlate",
-        grid=(blocks,),
-        out_shape=jax.ShapeDtypeStruct((blocks, 2, rows, inputs), bf16),
-        in_specs=[
-            pl.BlockSpec((CHUNKS, rows, 2 * STEP), lambda k: (0, k, 0)),
-            pl.BlockSpec(memory_space=pltpu.VMEM),
-        ],
-        out_specs=pl.BlockSpec((1, 2, rows, inputs), lambda k: (k, 0, 0, 0)),
-        compiler_params=pltpu.CompilerParams(vmem_limit_bytes=40 << 20),
-    )(spectra, spectra)
 
 
 def place_kernel(in_ref, mask_ref, out_ref, scratch):
@@ -180,13 +267,7 @@
 
 
 def per_device(voltages, fir_taps, band_start, band_count, subarray):
-    spectra = channelize(voltages, fir_taps, band_start, band_count)
-    spectra = lax.all_to_all(spectra, "chan", split_axis=0, concat_axis=0, tiled=True)
-    spectra = jnp.transpose(spectra, (2, 1, 0, 3, 4))
-    spectra = lax.all_to_all(spectra, "stn", split_axis=0, concat_axis=0, tiled=True)
-    spectra = jnp.transpose(spectra, (1, 0, 2, 3, 4)).reshape(CHUNKS, -1, 2 * STEP)
-    blocks = correlate(spectra, lax.axis_size("stn"))
-    blocks = lax.all_to_all(blocks, "stn", split_axis=0, concat_axis=0, tiled=True)
+    blocks = correlator(voltages, fir_taps, band_start, band_count)
     rows = blocks.shape[2]
     stations = jnp.repeat(subarray, 2)
     own = lax.dynamic_slice_in_dim(stations, lax.axis_index("stn") * rows, rows, 0)

time: 198 us -> 128 us (0.65)
  blocking collectives: 67.7 us -> 0 us
  Pallas kernels: 70.2 us -> 125 us
  waiting for transfers between devices: 52.4 us -> 0 us
  starting transfers between devices: 4.67 us -> 0 us
    all_to_all x2 -> x0, blocking collectives: 67.7 us -> none  [the longest x1 35.8 us: per_device(): lax.all_to_all(spectra, 'stn', split_axis=0, concat_axis=0, tiled=True)]
    pallas_call x2 -> x1, Pallas kernels: 58.2 us -> 114 us  [correlator(): pl.pallas_call(correlator_kernel, name='correlator', out_shape=jax.ShapeD...]
    all_to_all x1 -> x0, waiting for transfers between devices: 52.4 us -> none  [per_device(): lax.all_to_all(blocks, 'stn', split_axis=0, concat_axis=0, tiled=True)]
    all_to_all x1 -> x0, starting transfers between devices: 4.67 us -> none  [per_device(): lax.all_to_all(blocks, 'stn', split_axis=0, concat_axis=0, tiled=True)]
  transfers between devices with their start and end apart: 1 -> 0, of which waited for: 1 -> 0; matrix products, arithmetic and copies ran while one was open for 0% -> 0% of each run, Pallas kernels for 0% -> 0%
where the time goes in v2:
time: 128 us
  Pallas kernels  125 us (98%)
  local copies, waits for them, and re-layouts  3.23 us (3%)
    pallas_call x1, Pallas kernels, correlator(): pl.pallas_call(correlator_kernel, name='correlator', out_shape=jax.ShapeD...  114 us
    pallas_call x1, Pallas kernels, place(): pl.pallas_call(place_kernel, name='place', grid=(rows // 16,), out_shape=...  11.1 us

profile of v2, /device:TPU:0, one launch (start us, length us, event | category | flops | bytes accessed | tf_op | source)
XLA Modules:
  0.0 128.0 jit_solution(2895205844900580310)
XLA Ops:
  0.0 0.8 broadcast_in_dim.4
  0.8 0.2 reshape.8
  1.0 0.1 dynamic_slice.3
  1.1 0.1 compare_select_fusion.mask_ref
  1.2 113.6 %correlator.1.in_ref = bf16[16,2,64,1024]{3,2,1,0:T(8,128)(2,1)} custom-call(s32[8]{0:T(128)} %start_ref.1, s32[8]{0:T(128)} %count_ref.1, f32[12,1024]{1,0:T(8,128)} %taps_ref.1, bf16[2,8,535552]{2,1,0:T(8,128)(2,1)} %volt_hbm.1), custom_call_target="tpu_custom_call" | custom-call | tf_op jit(solution)/shard_map/correlator/pallas_call | solution.py:205
  114.8 0.0 copy-start
  114.8 2.2 %copy-done = bf16[16,2,64,1024]{3,2,1,0:T(8,128)(2,1)S(1)} copy-done((bf16[16,2,64,1024]{3,2,1,0:T(8,128)(2,1)S(1)}, bf16[16,2,64,1024]{3,2,1,0:T(8,128)(2,1)}, u32[]{:S(2)}) %copy-start) | copy-done | bytes 4194328
  117.0 11.1 %place.1 = f32[2048,1024]{1,0:T(8,128)} custom-call(bf16[16,2,64,1024]{3,2,1,0:T(8,128)(2,1)S(1)} %copy-done, f32[64,1024]{1,0:T(8,128)S(1)} %compare_select_fusion.mask_ref), custom_call_target="tpu_custom_call" | custom-call | tf_op jit(solution)/shard_map/place/pallas_call | solution.py:253
Async XLA Ops:
  114.8 2.2 %copy-start = (bf16[16,2,64,1024]{3,2,1,0:T(8,128)(2,1)S(1)}, bf16[16,2,64,1024]{3,2,1,0:T(8,128)(2,1)}, u32[]{:S(2)}) copy-start(bf16[16,2,64,1024]{3,2,1,0:T(8,128)(2,1)} %correlator.1.in_ref) | copy-start | bytes 12582916

commit v3 on v2

--- a/solution.py
+++ b/solution.py
@@ -1,3 +1,4 @@
+import functools
 import math
 
 import jax
@@ -14,6 +15,8 @@
 GROUPS = 8
 STEP = 128
 CHUNKS = SPECTRA // STEP
+ROOM = 384
+NSUB = 4
 f32 = jnp.float32
 bf16 = jnp.bfloat16
 MESH = pl.DeviceIdType.MESH
@@ -75,14 +78,26 @@
     lax.fori_loop(0, 16, strip, 0)
 
 
+def fill_picker(target_ref, picker):
+    target = target_ref[...]
+
+    def rows16(k, carry):
+        top = pl.multiple_of(k * 16, 16)
+        row = lax.broadcasted_iota(jnp.int32, (16, target.shape[1]), 0) + top
+        picker[pl.ds(top, 16), :] = jnp.where(row == target, f32(1), f32(0)).astype(bf16)
+        return carry
+
+    lax.fori_loop(0, NSUB * ROOM // 16, rows16, 0)
+
+
 def total_wait(ref, sem):
     pltpu.make_async_copy(ref, ref, sem).wait()
 
 
 def correlator_kernel(
-    start_ref, count_ref, taps_ref, volt_hbm, out_ref,
+    packed, start_ref, count_ref, taps_ref, target_ref, member_ref, volt_hbm, out_ref,
     volt, taps8, table, frames, mixed, sorted_, outgoing, passing, held, results,
-    volt_sem, send_a, recv_a, send_b, recv_b, send_c, recv_c,
+    picker, picked, summed, volt_sem, send_a, recv_a, send_b, recv_b, send_c, recv_c,
 ):
     chan, stn = lax.axis_index("chan"), lax.axis_index("stn")
     chans, stns = lax.axis_size("chan"), lax.axis_size("stn")
@@ -108,6 +123,8 @@
     for p in range(TAPS):
         taps8[p] = jnp.broadcast_to(taps_ref[p : p + 1, :], (8, NFFT))
     fill_table(start_ref, count_ref, table)
+    if packed:
+        fill_picker(target_ref, picker)
     pl.semaphore_wait(barrier, chans + stns - 2)
 
     def send_chan(c):
@@ -158,12 +175,62 @@
         return carry
 
     lax.fori_loop(0, CHUNKS, chunk, 0)
-    send_stn(CHUNKS - 1)
-    for c in range(CHUNKS):
-        total_wait(held.at[c], recv_b.at[c])
-
     inputs = stns * chans * 8
     rows = chans * 8
+    quad = 4
+
+    def pick(c):
+        total_wait(held.at[c], recv_b.at[c])
+        everyone = held[c].reshape(inputs, 2 * STEP)
+        picked[c] = jnp.dot(picker[...], everyone, preferred_element_type=f32).astype(bf16)
+
+    def add_up(c, b):
+        own = held[c, pl.ds(b * quad, quad)].reshape(quad * rows, 2 * STEP)
+        turned = jnp.concatenate([own[:, STEP:], -own[:, :STEP]], axis=1)
+        for o, left in enumerate((own, turned)):
+            wide = lax.dot_general(left, picked[c], NT, preferred_element_type=f32)
+            member = member_ref[pl.ds(pl.multiple_of(b * quad * rows, 8), quad * rows), :]
+            chosen = wide[:, 0:ROOM]
+            for n in range(1, NSUB):
+                chosen = jnp.where(member == n, wide[:, n * ROOM : (n + 1) * ROOM], chosen)
+            chosen = chosen.reshape(quad, rows, ROOM)
+            if c > 0:
+                chosen = chosen + summed[pl.ds(b * quad, quad), o]
+            if c < CHUNKS - 1:
+                summed[pl.ds(b * quad, quad), o] = chosen
+            else:
+                results[pl.ds(b * quad, quad), o] = chosen.astype(bf16)
+
+    def return_rows(k):
+        @pl.when(k != stn)
+        def _():
+            pltpu.make_async_remote_copy(
+                results.at[k], out_ref.at[stn], send_c, recv_c,
+                device_id=(chan, k), device_id_type=MESH,
+            ).start()
+
+        @pl.when(k == stn)
+        def _():
+            pltpu.make_async_copy(results.at[k], out_ref.at[stn], recv_c).start()
+
+    if packed:
+        send_stn(CHUNKS - 1)
+        for c in range(CHUNKS):
+            pick(c)
+
+            def add_block(s, carry, c=c):
+                b = (stn // quad + 1 + s) % (stns // quad)
+                add_up(c, b)
+                if c == CHUNKS - 1:
+                    for e in range(quad):
+                        return_rows(b * quad + e)
+                return carry
+
+            lax.fori_loop(0, stns // quad, add_block, 0)
+    else:
+        send_stn(CHUNKS - 1)
+        for c in range(CHUNKS):
+            total_wait(held.at[c], recv_b.at[c])
 
     def correlate(s, carry):
         k = (stn + 7 * (s + 1)) % stns
@@ -178,36 +245,28 @@
             total = part if total is None else total + part
         results[k] = total.reshape(2, rows, inputs).astype(bf16)
 
-        @pl.when(s < stns - 1)
-        def _():
-            pltpu.make_async_remote_copy(
-                results.at[k], out_ref.at[stn], send_c, recv_c,
-                device_id=(chan, k), device_id_type=MESH,
-            ).start()
-
-        @pl.when(s == stns - 1)
-        def _():
-            pltpu.make_async_copy(results.at[k], out_ref.at[stn], recv_c).start()
-
+        return_rows(k)
         return carry
 
-    lax.fori_loop(0, stns, correlate, 0)
+    if not packed:
+        lax.fori_loop(0, stns, correlate, 0)
     total_wait(outgoing.at[:, 0 : chans - 1], send_a)
     total_wait(held.at[:, 0 : stns - 1], send_b)
     total_wait(results.at[0 : stns - 1], send_c)
     total_wait(out_ref, recv_c)
 
 
-def correlator(voltages, fir_taps, band_start, band_count):
+def correlator(packed, voltages, fir_taps, band_start, band_count, target, member):
     chans, stns = lax.axis_size("chan"), lax.axis_size("stn")
     inputs = stns * chans * 8
-    blocks = (stns, 2, chans * 8, inputs)
+    blocks = (stns, 2, chans * 8, ROOM if packed else inputs)
     return pl.pallas_call(
-        correlator_kernel,
-        name="correlator",
+        functools.partial(correlator_kernel, packed),
+        name="correlator_packed" if packed else "correlator",
         out_shape=jax.ShapeDtypeStruct(blocks, bf16),
         in_specs=[pl.BlockSpec(memory_space=pltpu.SMEM)] * 2
-        + [pl.BlockSpec(memory_space=pltpu.VMEM), pl.BlockSpec(memory_space=pl.ANY)],
+        + [pl.BlockSpec(memory_space=pltpu.VMEM)] * 3
+        + [pl.BlockSpec(memory_space=pl.ANY)],
         out_specs=pl.BlockSpec(memory_space=pl.ANY),
         scratch_shapes=[
             pltpu.VMEM(voltages.shape, bf16),
@@ -220,6 +279,9 @@
             pltpu.VMEM((CHUNKS, chans, CMAX, 8, 2 * STEP), bf16),
             pltpu.VMEM((CHUNKS, stns, chans, 8, 2 * STEP), bf16),
             pltpu.VMEM(blocks, bf16),
+            pltpu.VMEM((NSUB * ROOM, inputs) if packed else (16, 128), bf16),
+            pltpu.VMEM((CHUNKS, NSUB * ROOM, 2 * STEP) if packed else (16, 128), bf16),
+            pltpu.VMEM(blocks if packed else (8, 128), f32),
             pltpu.SemaphoreType.DMA((CHUNKS + 1,)),
             pltpu.SemaphoreType.DMA,
             pltpu.SemaphoreType.DMA((CHUNKS,)),
@@ -229,9 +291,9 @@
             pltpu.SemaphoreType.DMA,
         ],
         compiler_params=pltpu.CompilerParams(
-            collective_id=0, has_side_effects=True, vmem_limit_bytes=58 << 20
+            collective_id=1 if packed else 0, has_side_effects=True, vmem_limit_bytes=58 << 20
         ),
-    )(band_start, band_count, fir_taps, voltages)
+    )(band_start, band_count, fir_taps, target, member, voltages)
 
 
 def place_kernel(in_ref, mask_ref, out_ref, scratch):
@@ -261,18 +323,85 @@
         ],
         out_specs=pl.BlockSpec((16 * 2 * slots, inputs), lambda b: (b, 0)),
         scratch_shapes=[pltpu.VMEM((8, 16 * 2 * slots, 128), f32)],
-        compiler_params=pltpu.CompilerParams(vmem_limit_bytes=40 << 20),
+        compiler_params=pltpu.CompilerParams(vmem_limit_bytes=60 << 20),
     )(blocks, mask)
     return flat.reshape(rows, 2, slots, inputs)
 
 
+def unpack_kernel(in_ref, place_ref, mask_ref, out_ref, scratch, spread):
+    slots, _, rows, room = in_ref.shape
+
+    @pl.when(pl.program_id(0) == 0)
+    def _():
+        place = place_ref[...]
+        row = lax.broadcasted_iota(jnp.int32, (room, place.shape[1]), 0)
+        spread[...] = jnp.where(row == place, f32(1), f32(0)).astype(bf16)
+
+    for q in range(slots):
+        for o in range(2):
+            values = in_ref[q, o].astype(f32)
+            for part in range(room // 128):
+                for half in range(rows // 8):
+                    scratch[part, pl.ds(half * 256 + o * 16 + q, 8, stride=32), :] = values[
+                        half * 8 : (half + 1) * 8, part * 128 : (part + 1) * 128
+                    ]
+    total = None
+    for part in range(room // 128):
+        product = jnp.dot(
+            scratch[part].astype(bf16), spread[part * 128 : (part + 1) * 128, :],
+            preferred_element_type=f32,
+        )
+        total = product if total is None else total + product
+    for i in range(rows):
+        out_ref[i * 32 : (i + 1) * 32, :] = total[i * 32 : (i + 1) * 32, :] * mask_ref[i : i + 1, :]
+
+
+def unpack(blocks, placing, mask):
+    slots, _, rows, room = blocks.shape
+    inputs = mask.shape[1]
+    flat = pl.pallas_call(
+        unpack_kernel,
+        name="unpack",
+        grid=(rows // 16,),
+        out_shape=jax.ShapeDtypeStruct((rows * 2 * slots, inputs), f32),
+        in_specs=[
+            pl.BlockSpec((slots, 2, 16, room), lambda b: (0, 0, b, 0)),
+            pl.BlockSpec((1, inputs), lambda b: (0, 0)),
+            pl.BlockSpec((16, inputs), lambda b: (b, 0)),
+        ],
+        out_specs=pl.BlockSpec((16 * 2 * slots, inputs), lambda b: (b, 0)),
+        scratch_shapes=[
+            pltpu.VMEM((room // 128, 16 * 2 * slots, 128), f32),
+            pltpu.VMEM((room, inputs), bf16),
+        ],
+        compiler_params=pltpu.CompilerParams(vmem_limit_bytes=60 << 20),
+    )(blocks, placing, mask)
+    return flat.reshape(rows, 2, slots, inputs)
+
+
 def per_device(voltages, fir_taps, band_start, band_count, subarray):
-    blocks = correlator(voltages, fir_taps, band_start, band_count)
-    rows = blocks.shape[2]
+    inputs = 2 * subarray.shape[0]
+    rows = inputs // lax.axis_size("stn")
+    same = subarray[:, None] == subarray[None, :]
+    index = jnp.arange(subarray.shape[0], dtype=jnp.int32)
+    before = jnp.sum((same & (index[:, None] < index[None, :])).astype(jnp.int32), axis=0)
+    fits = jnp.max(jnp.sum(same.astype(jnp.int32), axis=0)) <= ROOM // 2
     stations = jnp.repeat(subarray, 2)
+    placing = jnp.repeat(2 * before, 2) + jnp.arange(inputs, dtype=jnp.int32) % 2
+    target = (stations * ROOM + placing)[None, :]
+    member = stations[:, None]
     own = lax.dynamic_slice_in_dim(stations, lax.axis_index("stn") * rows, rows, 0)
     mask = (own[:, None] == stations[None, :]).astype(f32) / SPECTRA
-    return place(blocks, mask)
+
+    def packed_way():
+        blocks = correlator(True, voltages, fir_taps, band_start, band_count, target, member)
+        return unpack(blocks, placing[None, :], mask)
+
+    def full_way():
+        blocks = correlator(False, voltages, fir_taps, band_start, band_count, target, member)
+        return place(blocks, mask)
+
+    return lax.cond(fits, packed_way, full_way)
 
 
 def solution(mesh):

time: 128 us -> 108 us (0.84)
  the two profiles are of different devices: /device:TPU:0 before, /device:TPU:97 now
where the time goes in v3:
time: 108 us
  Pallas kernels  101 us (94%)
  local copies, waits for them, and re-layouts  3.04 us (3%)
  other arithmetic  3.01 us (3%)
    pallas_call x1, Pallas kernels, correlator(): pl.pallas_call(functools.partial(correlator_kernel, packed), name='correl...  93.3 us
    pallas_call x1, Pallas kernels, unpack(): pl.pallas_call(unpack_kernel, name='unpack', grid=(rows // 16,), out_shap...  7.46 us

profile of v3, /device:TPU:97, one launch (start us, length us, event | category | flops | bytes accessed | tf_op | source)
XLA Modules:
  0.0 107.7 jit_solution(11303490497028516277)
XLA Ops:
  0.0 0.7 broadcast_multiply_fusion.1
  0.7 1.0 convert_reduce_fusion
  1.7 0.6 reduce_max.9
  3.0 0.1 broadcast_in_dim.18
  3.1 0.2 reshape.65
  3.3 0.1 broadcast_in_dim.8
  3.4 0.2 mul.28
  3.6 0.8 broadcast_in_dim.19
  4.4 0.2 reshape.66
  4.6 0.2 broadcast_in_dim_reshape.4
  4.8 0.1 dynamic_slice.3
  4.9 0.1 compare_select_fusion
  5.0 102.7 %conditional.1 = (f32[64,2,16,1024]{3,2,1,0:T(8,128)}) conditional(s32[]{:T(128)} %convert_element_type.11, (s32[8]{0:T(128)}, s32[8]{0:T(128)}, f32[12,1024]{1,0:T(8,128)}, s32[1,1024]{1,0:T(1,128)S(1)}, s32[1024,1]{0,1:T(1,128)S(1)}, /*index=5*/bf16[2,8,535552]{2,1,0:T(8,128)(2,1)}, f32[64,1024]{1,0:T(8,128)S(1)}) %tuple.11, (s32[8]{0:T(128)}, ...), branch_computations={%region_3.4_spmd, %region_4.5_spmd.clone} | conditional | flops 6144 | bytes 45068 | solution.py:404
  5.2 0.2 reshape.70
  5.4 0.6 fusion
  6.0 1.0 copy.12.member_ref
  7.0 93.3 %correlator_packed.1.in_ref = bf16[16,2,64,384]{3,2,1,0:T(8,128)(2,1)} custom-call(s32[8]{0:T(128)} %get-tuple-element.69.start_ref, s32[8]{0:T(128)} %get-tuple-element.70.count_ref, f32[12,1024]{1,0:T(8,128)} %get-tuple-element.71.taps_ref, s32[1,1024]{1,0:T(1,128)S(1)} %get-tuple-element.72.target_ref, s32[1024,1]{1,0:T(8,128)} %copy.12.member_ref, ...), custom_call_target="tpu_custom_call" | custom-call | tf_op jit(solution)/shard_map/cond/branch_1_fun/correlator_packed/pallas_call | solution.py:263
  100.3 7.5 %unpack.1 = f32[2048,1024]{1,0:T(8,128)} custom-call(bf16[16,2,64,384]{3,2,1,0:T(8,128)(2,1)} %correlator_packed.1.in_ref, s32[1,1024]{1,0:T(1,128)} %bitcast.5, f32[64,1024]{1,0:T(8,128)S(1)} %get-tuple-element.75.mask_ref), custom_call_target="tpu_custom_call" | custom-call | tf_op jit(solution)/shard_map/cond/branch_1_fun/unpack/pallas_call | solution.py:362
  (4 shorter events, 0.0 us)

commit v4 on v2

v4 whole, which is shorter than its diff:
```python
import functools
import math

import jax
import jax.numpy as jnp
from jax import lax
from jax.experimental import pallas as pl
from jax.experimental.pallas import tpu as pltpu
from jax.sharding import PartitionSpec as P

NFFT = 1024
TAPS = 12
HALF = TAPS // 2
SPECTRA = 512
CMAX = 16
GROUPS = 8
STEP = 64
CHUNKS = SPECTRA // STEP
PAIRS = CHUNKS // 2
ROOM = 320
MAIN = 256
REST = ROOM - MAIN
WIDE = MAIN + 2 * REST
NSUB = 4
f32 = jnp.float32
bf16 = jnp.bfloat16
MESH = pl.DeviceIdType.MESH
NT = (((1,), (1,)), ((), ()))


def fill_table(start_ref, count_ref, table):
    lane = lax.broadcasted_iota(jnp.int32, (8, 128), 1)
    channel = lane % CMAX
    scale = jnp.zeros((8, 128), f32)
    for g in range(GROUPS):
        here = lane // CMAX == g
        channel = jnp.where(here, channel + start_ref[g], channel)
        live = here & (lane % CMAX < count_ref[g])
        scale = jnp.where(live, f32(1.0 / math.sqrt(NFFT)), scale)
    row = lax.broadcasted_iota(jnp.int32, (8, 128), 0)

    def rows16(k, carry):
        cosines, sines = [], []
        for half in range(2):
            phase = ((row + (k * 16 + half * 8)) * channel) & (NFFT - 1)
            angle = phase.astype(f32) * f32(2.0 * math.pi / NFFT)
            cosines.append(jnp.cos(angle) * scale)
            sines.append(jnp.sin(angle) * scale)
        cosine = jnp.concatenate(cosines, 0).astype(bf16)
        sine = jnp.concatenate(sines, 0)
        top = pl.multiple_of(k * 16, 16)
        low = pl.multiple_of(NFFT + k * 16, 16)
        table[pl.ds(top, 16), 0:128] = cosine
        table[pl.ds(top, 16), 128:256] = (-sine).astype(bf16)
        table[pl.ds(low, 16), 0:128] = sine.astype(bf16)
        table[pl.ds(low, 16), 128:256] = cosine
        return carry

    lax.fori_loop(0, NFFT // 16, rows16, 0)


def weighted(values, weights):
    total = values[0] * weights[0]
    for value, weight in zip(values[1:], weights[1:]):
        total = total + value * weight
    return total


def filter_chunk(volt, taps8, frames, first):
    def strip(n, carry):
        part = n // 8
        column = (n % 8) * 128
        lanes = pl.ds(pl.multiple_of(column, 128), 128)
        taps = [taps8[p, :, lanes] for p in range(TAPS)]
        sums = [taps8[TAPS + q, :, lanes] for q in range(HALF)]

        def sample(j):
            start = pl.multiple_of((first + j) * NFFT + column, 128)
            return volt[part, :, pl.ds(start, 128)].astype(f32)

        evens = [sample(2 * q) for q in range(HALF)]
        odds = [sample(2 * q + 1) for q in range(HALF - 1)]
        both = [e + o for e, o in zip(evens, odds)]
        b_now = weighted(evens, taps[1::2])
        for k in range(STEP // 2):
            odds.append(sample(2 * (k + HALF) - 1))
            both.append(evens[-1] + odds[-1])
            a_now = weighted(odds, taps[0::2])
            c_now = weighted(both, sums)
            evens = evens[1:] + [sample(2 * (k + HALF))]
            b_next = weighted(evens, taps[1::2])
            out = jnp.concatenate([c_now - (a_now + b_now), a_now + b_next], 0)
            frames[part, k * 16 : (k + 1) * 16, lanes] = out.astype(bf16)
            b_now = b_next
            odds = odds[1:]
            both = both[1:]
        return carry

    lax.fori_loop(0, 2 * NFFT // 128, strip, 0)


def transform_chunk(frames, table, mixed):
    product = jnp.dot(frames[0], table[0:NFFT, :], preferred_element_type=f32)
    product = product + jnp.dot(frames[1], table[NFFT:, :], preferred_element_type=f32)
    for o in range(2):
        mixed[o] = product[:, o * 128 : (o + 1) * 128]


def sort_chunk(mixed, sorted_, outgoing, c):
    for i in range(8):
        both = jnp.concatenate([mixed[o, pl.ds(i, STEP, stride=8), :] for o in range(2)], axis=0)
        sorted_[pl.ds(i, 128, stride=8), :] = both.T
    outgoing[c] = sorted_[...].reshape(outgoing.shape[1:]).astype(bf16)


def rank_members(stations, picker):
    inputs = stations.shape[1]

    def rows16(k, carry):
        top = pl.multiple_of(k * 16, 16)
        row = lax.broadcasted_iota(jnp.int32, (16, inputs), 0) + top
        column = lax.broadcasted_iota(jnp.int32, (16, inputs), 1)
        picker[pl.ds(top, 16), :] = jnp.where(row < column, f32(1), f32(0)).astype(bf16)
        return carry

    lax.fori_loop(0, inputs // 16, rows16, 0)
    kind = lax.broadcasted_iota(jnp.int32, (16, inputs), 0).astype(f32)
    onehot = jnp.where(kind == stations, f32(1), f32(0))
    before = jnp.dot(onehot.astype(bf16), picker[0:inputs, :], preferred_element_type=f32)
    return jnp.sum(onehot * before, axis=0, keepdims=True)


def fill_picker(target, picker):
    def rows16(k, carry):
        top = pl.multiple_of(k * 16, 16)
        column = top % WIDE
        base = (top // WIDE) * ROOM + column - jnp.where(column >= ROOM, REST, 0)
        row = lax.broadcasted_iota(jnp.int32, (16, target.shape[1]), 0) + base
        picker[pl.ds(top, 16), :] = jnp.where(row.astype(f32) == target, f32(1), f32(0)).astype(bf16)
        return carry

    lax.fori_loop(0, NSUB * WIDE // 16, rows16, 0)


def fill_turn(turn):
    row = lax.broadcasted_iota(jnp.int32, turn.shape, 0)
    column = lax.broadcasted_iota(jnp.int32, turn.shape, 1)
    low = column % (2 * STEP) < STEP
    ones = jnp.where(low & (row == column + STEP), f32(1), f32(0))
    turn[...] = (ones - jnp.where(~low & (row == column - STEP), f32(1), f32(0))).astype(bf16)


def total_wait(ref, sem):
    pltpu.make_async_copy(ref, ref, sem).wait()


def correlator_kernel(
    packed, start_ref, count_ref, taps_ref, stations_ref, volt_hbm, out_ref, placing_ref,
    volt, taps8, table, frames, mixed, sorted_, outgoing, passing, held, results,
    turn, picker, member, picked, summed, volt_sem, send_a, recv_a, send_b, recv_b, send_c, recv_c,
):
    chan, stn = lax.axis_index("chan"), lax.axis_index("stn")
    chans, stns = lax.axis_size("chan"), lax.axis_size("stn")

    def volt_copy(c, first):
        low = first * NFFT
        wide = STEP * NFFT
        span = pl.ds(pl.multiple_of(low, 128), wide)
        return pltpu.make_async_copy(volt_hbm.at[:, :, span], volt.at[:, :, span], volt_sem.at[c])

    halo = pl.ds(SPECTRA * NFFT, (TAPS - 1) * NFFT)
    halo_copy = pltpu.make_async_copy(volt_hbm.at[:, :, halo], volt.at[:, :, halo], volt_sem.at[CHUNKS])
    for c in range(CHUNKS):
        volt_copy(c, c * STEP).start()
    halo_copy.start()

    barrier = pltpu.get_barrier_semaphore()
    for d in range(1, chans):
        pl.semaphore_signal(barrier, inc=1, device_id=((chan + d) % chans, stn), device_id_type=MESH)
    for d in range(1, stns):
        pl.semaphore_signal(barrier, inc=1, device_id=(chan, (stn + d) % stns), device_id_type=MESH)

    for p in range(TAPS):
        taps8[p] = jnp.broadcast_to(taps_ref[p : p + 1, :], (8, NFFT))
    for q in range(HALF):
        taps8[TAPS + q] = taps8[2 * q] + taps8[2 * q + 1]
    fill_table(start_ref, count_ref, table)
    pl.semaphore_wait(barrier, chans + stns - 2)

    def send_chan(c):
        for d in range(1, chans):
            to = (chan + d) % chans
            pltpu.make_async_remote_copy(
                outgoing.at[c, to], passing.at[c, chan], send_a, recv_a.at[c],
                device_id=(to, stn), device_id_type=MESH,
            ).start()
        pltpu.make_async_copy(outgoing.at[c, chan], passing.at[c, chan], recv_a.at[c]).start()

    def held_part(c):
        half = pl.ds(pl.multiple_of((c % 2) * 2 * STEP, 128), 2 * STEP)
        return held.at[c // 2, :, :, :, half]

    def send_stn(c):
        total_wait(passing.at[c], recv_a.at[c])
        for d in range(1, stns):
            to = (stn + d) % stns
            pltpu.make_async_remote_copy(
                passing.at[c, :, to], held_part(c).at[stn], send_b, recv_b.at[c],
                device_id=(chan, to), device_id_type=MESH,
            ).start()
        pltpu.make_async_copy(passing.at[c, :, stn], held_part(c).at[stn], recv_b.at[c]).start()

    volt_copy(0, 0).wait()

    def chunk(c, carry):
        @pl.when(c < CHUNKS - 1)
        def _():
            volt_copy(c + 1, (c + 1) * STEP).wait()

        @pl.when(c == CHUNKS - 1)
        def _():
            halo_copy.wait()

        filter_chunk(volt, taps8, frames, c * STEP)
        transform_chunk(frames, table, mixed)
        sort_chunk(mixed, sorted_, outgoing, c)
        send_chan(c)

        @pl.when(c > 1)
        def _():
            send_stn(c - 2)

        return carry

    lax.fori_loop(0, CHUNKS, chunk, 0)
    fill_turn(turn)
    if packed:
        stations = stations_ref[...]
        placing = rank_members(stations, picker)
        placing_ref[...] = placing
        fill_picker(stations * ROOM + placing, picker)
        for b in range(stations.shape[1] // 128):
            strip = jnp.broadcast_to(stations[:, b * 128 : (b + 1) * 128], (128, 128))
            member[b * 128 : (b + 1) * 128, :] = strip.T
    else:
        placing_ref[...] = jnp.zeros_like(placing_ref)
    send_stn(CHUNKS - 2)

    inputs = stns * chans * 8
    rows = chans * 8
    quad = 4

    def arrived(c):
        for half in range(2):
            total_wait(held.at[c, :, :, :, 0 : 2 * STEP], recv_b.at[2 * c + half])

    def pick(c):
        arrived(c)
        everyone = held[c].reshape(inputs, 4 * STEP)
        picked[c] = jnp.dot(picker[...], everyone, preferred_element_type=f32).astype(bf16)

    def add_up(c, b):
        own = held[c, pl.ds(b * quad, quad)].reshape(quad * rows, 4 * STEP)
        turned = jnp.dot(own, turn[...], preferred_element_type=f32).astype(bf16)
        both = jnp.concatenate([own, turned], axis=0)
        product = lax.dot_general(both, picked[c], NT, preferred_element_type=f32)
        kinds = member[pl.ds(pl.multiple_of(b * quad * rows, 8), quad * rows), :]
        kinds = jnp.concatenate([kinds] * (WIDE // 128), axis=1)
        parts = []
        for o in range(2):
            wide = product[o * quad * rows : (o + 1) * quad * rows]
            chosen = wide[:, 0:WIDE]
            for n in range(1, NSUB):
                chosen = jnp.where(kinds == n, wide[:, n * WIDE : (n + 1) * WIDE], chosen)
            if c > 0:
                chosen = chosen + summed[b, o]
            if c < PAIRS - 1:
                summed[b, o] = chosen
            parts.append(chosen)
        if c == PAIRS - 1:
            lane = lax.broadcasted_iota(jnp.int32, (quad * rows, 2 * REST), 1)
            rest = jnp.where(lane < REST, parts[0][:, MAIN:], parts[1][:, MAIN:])
            full = jnp.concatenate([parts[0][:, :MAIN], parts[1][:, :MAIN], rest], axis=1)
            results[pl.ds(b * quad, quad)] = full.astype(bf16).reshape(quad, rows, 2 * ROOM)

    def return_rows(k):
        @pl.when(k != stn)
        def _():
            pltpu.make_async_remote_copy(
                results.at[k], out_ref.at[stn], send_c, recv_c,
                device_id=(chan, k), device_id_type=MESH,
            ).start()

        @pl.when(k == stn)
        def _():
            pltpu.make_async_copy(results.at[k], out_ref.at[stn], recv_c).start()

    def add_pair(c):
        pick(c)

        def add_block(s, carry):
            b = (stn // quad + 1 + s) % (stns // quad)
            add_up(c, b)
            if c == PAIRS - 1:
                for e in range(quad):
                    return_rows(b * quad + e)
            return carry

        lax.fori_loop(0, stns // quad, add_block, 0)

    if packed:
        add_pair(0)
        send_stn(CHUNKS - 1)
        for c in range(1, PAIRS):
            add_pair(c)
    else:
        send_stn(CHUNKS - 1)
        for c in range(PAIRS):
            arrived(c)

    def correlate(s, carry):
        k = (stn + 7 * (s + 1)) % stns
        total = None
        for c in range(PAIRS):
            own = held[c, k].reshape(rows, 4 * STEP)
            turned = jnp.dot(own, turn[...], preferred_element_type=f32).astype(bf16)
            both = jnp.concatenate([own, turned], axis=0)
            part = lax.dot_general(
                both, held[c].reshape(inputs, 4 * STEP), NT, preferred_element_type=f32
            )
            total = part if total is None else total + part
        results[k] = total.reshape(2, rows, inputs).astype(bf16)

        return_rows(k)
        return carry

    if not packed:
        lax.fori_loop(0, stns, correlate, 0)
    total_wait(outgoing.at[:, 0 : chans - 1], send_a)
    total_wait(held.at[:, 0 : stns - 1], send_b)
    total_wait(results.at[0 : stns - 1], send_c)
    total_wait(out_ref, recv_c)


def correlator(packed, voltages, fir_taps, band_start, band_count, stations):
    chans, stns = lax.axis_size("chan"), lax.axis_size("stn")
    inputs = stns * chans * 8
    blocks = (stns, chans * 8, 2 * ROOM) if packed else (stns, 2, chans * 8, inputs)
    sums = (stns // 4, 2, chans * 32, WIDE)
    return pl.pallas_call(
        functools.partial(correlator_kernel, packed),
        name="correlator_packed" if packed else "correlator",
        out_shape=(
            jax.ShapeDtypeStruct(blocks, bf16),
            jax.ShapeDtypeStruct((1, inputs), f32),
        ),
        in_specs=[pl.BlockSpec(memory_space=pltpu.SMEM)] * 2
        + [pl.BlockSpec(memory_space=pltpu.VMEM)] * 2
        + [pl.BlockSpec(memory_space=pl.ANY)],
        out_specs=(pl.BlockSpec(memory_space=pl.ANY), pl.BlockSpec(memory_space=pltpu.VMEM)),
        scratch_shapes=[
            pltpu.VMEM(voltages.shape, bf16),
            pltpu.VMEM((TAPS + HALF, 8, NFFT), f32),
            pltpu.VMEM((2 * NFFT, 256), bf16),
            pltpu.VMEM((2, STEP * 8, NFFT), bf16),
            pltpu.VMEM((2, STEP * 8, 128), f32),
            pltpu.VMEM((128 * 8, 128), f32),
            pltpu.VMEM((CHUNKS, chans, CMAX, 8, 2 * STEP), bf16),
            pltpu.VMEM((CHUNKS, chans, CMAX, 8, 2 * STEP), bf16),
            pltpu.VMEM((PAIRS, stns, chans, 8, 4 * STEP), bf16),
            pltpu.VMEM(blocks, bf16),
            pltpu.VMEM((4 * STEP, 4 * STEP), bf16),
            pltpu.VMEM((NSUB * WIDE, inputs) if packed else (16, 128), bf16),
            pltpu.VMEM((inputs, 128) if packed else (8, 128), f32),
            pltpu.VMEM((PAIRS, NSUB * WIDE, 4 * STEP) if packed else (16, 128), bf16),
            pltpu.VMEM(sums if packed else (8, 128), f32),
            pltpu.SemaphoreType.DMA((CHUNKS + 1,)),
            pltpu.SemaphoreType.DMA,
            pltpu.SemaphoreType.DMA((CHUNKS,)),
            pltpu.SemaphoreType.DMA,
            pltpu.SemaphoreType.DMA((CHUNKS,)),
            pltpu.SemaphoreType.DMA,
            pltpu.SemaphoreType.DMA,
        ],
        compiler_params=pltpu.CompilerParams(
            collective_id=1 if packed else 0, has_side_effects=True, vmem_limit_bytes=58 << 20
        ),
    )(band_start, band_count, fir_taps, stations, voltages)


def place_kernel(in_ref, mask_ref, out_ref, scratch):
    mask = mask_ref[...]
    for q in range(CMAX):
        for o in range(2):
            values = in_ref[q, o].astype(f32) * mask
            for part in range(8):
                for half in range(2):
                    scratch[part, pl.ds(half * 256 + o * 16 + q, 8, stride=32), :] = values[
                        half * 8 : (half + 1) * 8, part * 128 : (part + 1) * 128
                    ]
    for part in range(8):
        out_ref[:, part * 128 : (part + 1) * 128] = scratch[part]


def place(blocks, mask):
    slots, _, rows, inputs = blocks.shape
    flat = pl.pallas_call(
        place_kernel,
        name="place",
        grid=(rows // 16,),
        out_shape=jax.ShapeDtypeStruct((rows * 2 * slots, inputs), f32),
        in_specs=[
            pl.BlockSpec((slots, 2, 16, inputs), lambda b: (0, 0, b, 0)),
            pl.BlockSpec((16, inputs), lambda b: (b, 0)),
        ],
        out_specs=pl.BlockSpec((16 * 2 * slots, inputs), lambda b: (b, 0)),
        scratch_shapes=[pltpu.VMEM((8, 16 * 2 * slots, 128), f32)],
        compiler_params=pltpu.CompilerParams(vmem_limit_bytes=60 << 20),
    )(blocks, mask)
    return flat.reshape(rows, 2, slots, inputs)


def unpack_kernel(own_ref, in_ref, place_ref, stations_ref, out_ref, scratch, spread):
    slots, rows, _ = in_ref.shape

    @pl.when(pl.program_id(0) == 0)
    def _():
        place = place_ref[...]
        row = lax.broadcasted_iota(jnp.int32, (WIDE, place.shape[1]), 0)
        for o in range(2):
            mine = (row < MAIN) | ((row >= MAIN + o * REST) & (row < ROOM + o * REST))
            rank = jnp.where(mine, jnp.where(row < MAIN, row, row - o * REST), -1)
            spread[o] = jnp.where(rank.astype(f32) == place, f32(1), f32(0)).astype(bf16)

    for q in range(slots):
        values = in_ref[q].astype(f32)
        for part in range(2 * ROOM // 128):
            for half in range(rows // 8):
                scratch[part, pl.ds(half * 8 * slots + q, 8, stride=slots), :] = values[
                    half * 8 : (half + 1) * 8, part * 128 : (part + 1) * 128
                ]
    stations = stations_ref[...]
    masks = []
    for i in range(rows // 2):
        kind = own_ref[pl.program_id(0) * (rows // 2) + i].astype(f32)
        masks.append(jnp.where(stations == kind, f32(1.0 / SPECTRA), f32(0)))
    for o in range(2):
        packed = [scratch[part].astype(bf16) for part in (2 * o, 2 * o + 1, 4)]
        total = jnp.dot(jnp.concatenate(packed, axis=1), spread[o], preferred_element_type=f32)
        for i in range(rows):
            out_ref[i, o] = total[i * slots : (i + 1) * slots, :] * masks[i // 2]


def unpack(blocks, placing, stations, own):
    slots, rows, _ = blocks.shape
    inputs = stations.shape[1]
    return pl.pallas_call(
        unpack_kernel,
        name="unpack",
        grid=(rows // 16,),
        out_shape=jax.ShapeDtypeStruct((rows, 2, slots, inputs), f32),
        in_specs=[
            pl.BlockSpec(memory_space=pltpu.SMEM),
            pl.BlockSpec((slots, 16, 2 * ROOM), lambda b: (0, b, 0)),
            pl.BlockSpec((1, inputs), lambda b: (0, 0)),
            pl.BlockSpec((1, inputs), lambda b: (0, 0)),
        ],
        out_specs=pl.BlockSpec((16, 2, slots, inputs), lambda b: (b, 0, 0, 0)),
        scratch_shapes=[
            pltpu.VMEM((2 * ROOM // 128, 16 * slots, 128), f32),
            pltpu.VMEM((2, WIDE, inputs), bf16),
        ],
        compiler_params=pltpu.CompilerParams(vmem_limit_bytes=60 << 20),
    )(own, blocks, placing, stations)


def per_device(voltages, fir_taps, band_start, band_count, subarray):
    count = subarray.shape[0] // lax.axis_size("stn")
    kinds = jnp.arange(NSUB, dtype=jnp.int32)
    sizes = jnp.sum((subarray[None, :] == kinds[:, None]).astype(jnp.int32), axis=1)
    fits = jnp.max(sizes) <= ROOM // 2
    own = lax.dynamic_slice_in_dim(subarray, lax.axis_index("stn") * count, count, 0)
    stations = jnp.repeat(subarray.astype(f32), 2)[None, :]

    def packed_way():
        blocks, placing = correlator(True, voltages, fir_taps, band_start, band_count, stations)
        return unpack(blocks, placing, stations, own)

    def full_way():
        blocks, _ = correlator(False, voltages, fir_taps, band_start, band_count, stations)
        own_rows = jnp.repeat(own, 2)[:, None].astype(f32)
        return place(blocks, (own_rows == stations).astype(f32) / SPECTRA)

    return lax.cond(fits, packed_way, full_way)


def solution(mesh):
    in_specs = (P(None, ("stn", "chan"), None), P(), P(), P(), P())
    out_specs = P("stn", None, "chan", None)
    return jax.shard_map(
        per_device, mesh=mesh, in_specs=in_specs, out_specs=out_specs, check_vma=False
    )
```

time: 128 us -> 89.6 us (0.70)
  Pallas kernels: 125 us -> 83.4 us
  other arithmetic: 0.09 us -> 2.12 us
    pallas_call x2, Pallas kernels: 125 us -> 83.4 us  [the longest x1 76.7 us: correlator(): pl.pallas_call(functools.partial(correlator_kernel, packed), name='correl...]
    unnamed x2 -> x0, local copies, waits for them, and re-layouts: 2.18 us -> none
where the time goes in v4:
time: 89.6 us; the launch traced here: 88.5 us
  Pallas kernels  83.4 us (93%)
  local copies, waits for them, and re-layouts  2.23 us (2%)
  other arithmetic  2.12 us (2%)
    pallas_call x1, Pallas kernels, correlator(): pl.pallas_call(functools.partial(correlator_kernel, packed), name='correl...  76.7 us
    pallas_call x1, Pallas kernels, unpack(): pl.pallas_call(unpack_kernel, name='unpack', grid=(rows // 16,), out_shap...  6.74 us

profile of v4, /device:TPU:0, one launch (start us, length us, event | category | flops | bytes accessed | tf_op | source)
XLA Modules:
  0.0 88.5 jit_solution(7599372210567555569)
XLA Ops:
  0.0 0.8 convert_reduce_fusion
  0.8 0.6 reduce_max.9
  2.1 0.7 convert_element_type.24
  2.8 85.7 %conditional.1 = (f32[64,2,16,1024]{3,2,1,0:T(8,128)}) conditional(s32[]{:T(128)} %convert_element_type.23, (s32[8]{0:T(128)}, s32[8]{0:T(128)}, f32[12,1024]{1,0:T(8,128)}, f32[512]{0:T(512)S(1)}, bf16[2,8,535552]{2,1,0:T(8,128)(2,1)}, /*index=5*/s32[512]{0:T(512)}, s32[]{:T(128)}, s32[]{:T(128)}, s32[]{:T(128)}, s32[]{:T(128)}) %tuple.16, ...), branch_computations={%region_2.0_spmd.clone, %region_3.0_spmd.clone} | conditional | flops 131107 | bytes 290222 | solution.py:494
  2.8 1.3 %dynamic_slice.7.own_ref = s32[32]{0:T(128)} dynamic-slice(s32[512]{0:T(512)} %get-tuple-element.109, s32[]{:T(128)S(6)} %select_n.7), dynamic_slice_sizes={32} | dynamic-slice | bytes 260 | tf_op jit(solution)/shard_map/dynamic_slice | solution.py:482
  4.1 0.1 broadcast_in_dim.13
  4.2 0.8 broadcast_in_dim_reshape.7.stations_ref
  5.0 76.7 %correlator_packed.1 = (bf16[16,64,640]{2,1,0:T(8,128)(2,1)}, f32[1,1024]{1,0:T(1,128)}) custom-call(s32[8]{0:T(128)} %get-tuple-element.110.start_ref, s32[8]{0:T(128)} %get-tuple-element.111.count_ref, f32[12,1024]{1,0:T(8,128)} %get-tuple-element.112.taps_ref, f32[1,1024]{1,0:T(1,128)} %broadcast_in_dim_reshape.7.stations_ref, ...), custom_call_target="tpu_custom_call" | custom-call | tf_op jit(solution)/shard_map/cond/branch_1_fun/correlator_packed/pallas_call | solution.py:350
  81.7 6.7 %unpack.1 = f32[64,2,16,1024]{3,2,1,0:T(8,128)} custom-call(s32[32]{0:T(128)} %dynamic_slice.7.own_ref, bf16[16,64,640]{2,1,0:T(8,128)(2,1)} %get-tuple-element.107.in_ref, f32[1,1024]{1,0:T(1,128)} %get-tuple-element.108.place_ref, f32[1,1024]{1,0:T(1,128)} %broadcast_in_dim_reshape.7.stations_ref), custom_call_target="tpu_custom_call" | custom-call | tf_op jit(solution)/shard_map/cond/branch_1_fun/unpack/pallas_call | solution.py:457

commit v5 on v4

--- a/solution.py
+++ b/solution.py
@@ -66,42 +66,61 @@
     return total
 
 
+def once(function):
+    known = {}
+
+    def get(k):
+        if k not in known:
+            known[k] = function(k)
+        return known[k]
+
+    return get
+
+
+def halved(stream, taps, sums):
+    reach = range(len(sums))
+    odds = lambda m: stream(2 * m + 1)
+    evens = lambda m: stream(2 * m)
+    both = once(lambda m: evens(m) + odds(m))
+    a = once(lambda m: weighted([odds(m + q) for q in reach], taps[0::2]))
+    b = once(lambda m: weighted([evens(m + q) for q in reach], taps[1::2]))
+    c = once(lambda m: weighted([both(m + q) for q in reach], sums))
+
+    def output(k):
+        m = k // 2
+        return c(m) - (a(m) + b(m)) if k % 2 == 0 else a(m) + b(m + 1)
+
+    return once(output)
+
+
 def filter_chunk(volt, taps8, frames, first):
     def strip(n, carry):
         part = n // 8
         column = (n % 8) * 128
         lanes = pl.ds(pl.multiple_of(column, 128), 128)
-        taps = [taps8[p, :, lanes] for p in range(TAPS)]
-        sums = [taps8[TAPS + q, :, lanes] for q in range(HALF)]
+        taps = [taps8[p, :, lanes] for p in range(TAPS + 5 * HALF // 2)]
 
         def sample(j):
             start = pl.multiple_of((first + j) * NFFT + column, 128)
             return volt[part, :, pl.ds(start, 128)].astype(f32)
 
-        evens = [sample(2 * q) for q in range(HALF)]
-        odds = [sample(2 * q + 1) for q in range(HALF - 1)]
-        both = [e + o for e, o in zip(evens, odds)]
-        b_now = weighted(evens, taps[1::2])
+        odds = once(lambda k: sample(2 * k + 1))
+        evens = once(lambda k: sample(2 * k))
+        both = once(lambda k: evens(k) + odds(k))
+        third = HALF // 2
+        a = halved(odds, taps[0:TAPS:2], taps[TAPS + HALF : TAPS + HALF + third])
+        b = halved(evens, taps[1:TAPS:2], taps[TAPS + HALF + third : TAPS + HALF + 2 * third])
+        c = halved(both, taps[TAPS : TAPS + HALF], taps[TAPS + HALF + 2 * third :])
         for k in range(STEP // 2):
-            odds.append(sample(2 * (k + HALF) - 1))
-            both.append(evens[-1] + odds[-1])
-            a_now = weighted(odds, taps[0::2])
-            c_now = weighted(both, sums)
-            evens = evens[1:] + [sample(2 * (k + HALF))]
-            b_next = weighted(evens, taps[1::2])
-            out = jnp.concatenate([c_now - (a_now + b_now), a_now + b_next], 0)
-            frames[part, k * 16 : (k + 1) * 16, lanes] = out.astype(bf16)
-            b_now = b_next
-            odds = odds[1:]
-            both = both[1:]
+            out = jnp.concatenate([c(k) - (a(k) + b(k)), a(k) + b(k + 1)], 0)
+            frames[k * 16 : (k + 1) * 16, pl.ds(pl.multiple_of(n * 128, 128), 128)] = out.astype(bf16)
         return carry
 
     lax.fori_loop(0, 2 * NFFT // 128, strip, 0)
 
 
 def transform_chunk(frames, table, mixed):
-    product = jnp.dot(frames[0], table[0:NFFT, :], preferred_element_type=f32)
-    product = product + jnp.dot(frames[1], table[NFFT:, :], preferred_element_type=f32)
+    product = jnp.dot(frames[...], table[...], preferred_element_type=f32)
     for o in range(2):
         mixed[o] = product[:, o * 128 : (o + 1) * 128]
 
@@ -184,6 +203,12 @@
         taps8[p] = jnp.broadcast_to(taps_ref[p : p + 1, :], (8, NFFT))
     for q in range(HALF):
         taps8[TAPS + q] = taps8[2 * q] + taps8[2 * q + 1]
+    third = HALF // 2
+    for q in range(third):
+        low, high = TAPS + 2 * q, TAPS + 2 * q + 1
+        taps8[TAPS + HALF + q] = taps8[4 * q] + taps8[4 * q + 2]
+        taps8[TAPS + HALF + third + q] = taps8[4 * q + 1] + taps8[4 * q + 3]
+        taps8[TAPS + HALF + 2 * third + q] = taps8[low] + taps8[high]
     fill_table(start_ref, count_ref, table)
     pl.semaphore_wait(barrier, chans + stns - 2)
 
@@ -360,9 +385,9 @@
         out_specs=(pl.BlockSpec(memory_space=pl.ANY), pl.BlockSpec(memory_space=pltpu.VMEM)),
         scratch_shapes=[
             pltpu.VMEM(voltages.shape, bf16),
-            pltpu.VMEM((TAPS + HALF, 8, NFFT), f32),
+            pltpu.VMEM((TAPS + 5 * HALF // 2, 8, NFFT), f32),
             pltpu.VMEM((2 * NFFT, 256), bf16),
-            pltpu.VMEM((2, STEP * 8, NFFT), bf16),
+            pltpu.VMEM((STEP * 8, 2 * NFFT), bf16),
             pltpu.VMEM((2, STEP * 8, 128), f32),
             pltpu.VMEM((128 * 8, 128), f32),
             pltpu.VMEM((CHUNKS, chans, CMAX, 8, 2 * STEP), bf16),
@@ -420,17 +445,19 @@
     return flat.reshape(rows, 2, slots, inputs)
 
 
-def unpack_kernel(own_ref, in_ref, place_ref, stations_ref, out_ref, scratch, spread):
+def unpack_kernel(subarray_ref, in_ref, place_ref, stations_ref, out_ref, scratch, spread):
     slots, rows, _ = in_ref.shape
 
     @pl.when(pl.program_id(0) == 0)
     def _():
         place = place_ref[...]
-        row = lax.broadcasted_iota(jnp.int32, (WIDE, place.shape[1]), 0)
+        row = lax.broadcasted_iota(jnp.int32, (MAIN, place.shape[1]), 0).astype(f32)
+        main = jnp.where(row == place, f32(1), f32(0)).astype(bf16)
+        rest = jnp.where(row[:REST] + MAIN == place, f32(1), f32(0)).astype(bf16)
         for o in range(2):
-            mine = (row < MAIN) | ((row >= MAIN + o * REST) & (row < ROOM + o * REST))
-            rank = jnp.where(mine, jnp.where(row < MAIN, row, row - o * REST), -1)
-            spread[o] = jnp.where(rank.astype(f32) == place, f32(1), f32(0)).astype(bf16)
+            spread[o, 0:MAIN] = main
+            spread[o, MAIN + o * REST : ROOM + o * REST] = rest
+            spread[o, ROOM - o * REST : WIDE - o * REST] = jnp.zeros_like(rest)
 
     for q in range(slots):
         values = in_ref[q].astype(f32)
@@ -441,8 +468,9 @@
                 ]
     stations = stations_ref[...]
     masks = []
+    first = (lax.axis_index("stn") * pl.num_programs(0) + pl.program_id(0)) * (rows // 2)
     for i in range(rows // 2):
-        kind = own_ref[pl.program_id(0) * (rows // 2) + i].astype(f32)
+        kind = subarray_ref[first + i].astype(f32)
         masks.append(jnp.where(stations == kind, f32(1.0 / SPECTRA), f32(0)))
     for o in range(2):
         packed = [scratch[part].astype(bf16) for part in (2 * o, 2 * o + 1, 4)]
@@ -451,7 +479,7 @@
             out_ref[i, o] = total[i * slots : (i + 1) * slots, :] * masks[i // 2]
 
 
-def unpack(blocks, placing, stations, own):
+def unpack(blocks, placing, stations, subarray):
     slots, rows, _ = blocks.shape
     inputs = stations.shape[1]
     return pl.pallas_call(
@@ -471,27 +499,49 @@
             pltpu.VMEM((2, WIDE, inputs), bf16),
         ],
         compiler_params=pltpu.CompilerParams(vmem_limit_bytes=60 << 20),
-    )(own, blocks, placing, stations)
+    )(subarray, blocks, placing, stations)
+
+
+def prepare_kernel(subarray_ref, stations_ref, fits_ref):
+    kinds = jnp.broadcast_to(subarray_ref[...], (16, subarray_ref.shape[1])).astype(f32)
+    row = lax.broadcasted_iota(jnp.int32, (16, subarray_ref.shape[1]), 0).astype(f32)
+    sizes = jnp.sum(jnp.where(kinds == row, f32(1), f32(0)), axis=1, keepdims=True)
+    fits_ref[0] = jnp.where(jnp.max(sizes) * 2 <= ROOM, 1, 0)
+    shape = (subarray_ref.shape[1], stations_ref.shape[1])
+    station = lax.broadcasted_iota(jnp.int32, shape, 0) * 2
+    column = lax.broadcasted_iota(jnp.int32, shape, 1)
+    twice = jnp.where((column - station == 0) | (column - station == 1), f32(1), f32(0))
+    stations = jnp.dot(kinds.astype(bf16), twice.astype(bf16), preferred_element_type=f32)
+    stations_ref[...] = stations[0:1]
+
+
+def prepare(subarray):
+    return pl.pallas_call(
+        prepare_kernel,
+        name="prepare",
+        out_shape=(
+            jax.ShapeDtypeStruct((1, 2 * subarray.shape[0]), f32),
+            jax.ShapeDtypeStruct((1,), jnp.int32),
+        ),
+        in_specs=[pl.BlockSpec(memory_space=pltpu.VMEM)],
+        out_specs=(pl.BlockSpec(memory_space=pltpu.VMEM), pl.BlockSpec(memory_space=pltpu.SMEM)),
+    )(subarray[None, :])
 
 
 def per_device(voltages, fir_taps, band_start, band_count, subarray):
-    count = subarray.shape[0] // lax.axis_size("stn")
-    kinds = jnp.arange(NSUB, dtype=jnp.int32)
-    sizes = jnp.sum((subarray[None, :] == kinds[:, None]).astype(jnp.int32), axis=1)
-    fits = jnp.max(sizes) <= ROOM // 2
-    own = lax.dynamic_slice_in_dim(subarray, lax.axis_index("stn") * count, count, 0)
-    stations = jnp.repeat(subarray.astype(f32), 2)[None, :]
+    stations, fits = prepare(subarray)
 
     def packed_way():
         blocks, placing = correlator(True, voltages, fir_taps, band_start, band_count, stations)
-        return unpack(blocks, placing, stations, own)
+        return unpack(blocks, placing, stations, subarray)
 
     def full_way():
         blocks, _ = correlator(False, voltages, fir_taps, band_start, band_count, stations)
-        own_rows = jnp.repeat(own, 2)[:, None].astype(f32)
-        return place(blocks, (own_rows == stations).astype(f32) / SPECTRA)
-
-    return lax.cond(fits, packed_way, full_way)
+        rows = blocks.shape[2]
+        own = lax.dynamic_slice_in_dim(stations, lax.axis_index("stn") * rows, rows, 1)
+        return place(blocks, (own.T == stations).astype(f32) / SPECTRA)
+
+    return lax.cond(fits[0] == 1, packed_way, full_way)
 
 
 def solution(mesh):

time: 89.6 us -> 86.3 us (0.963)
  local copies, waits for them, and re-layouts: 2.23 us -> 0.01 us
  other arithmetic: 2.12 us -> 0 us
    pallas_call x0 -> x1, Pallas kernels: none -> 1.66 us  [prepare(): pl.pallas_call(prepare_kernel, name='prepare', out_shape=(jax.ShapeDtypeS...]
    dynamic_slice x1 -> x0, local copies, waits for them, and re-layouts: 1.33 us -> none  [per_device(): lax.dynamic_slice_in_dim(subarray, lax.axis_index('stn') * count, count, 0)]
    pallas_call x1, Pallas kernels: 76.7 us -> 75.8 us  [correlator(): pl.pallas_call(functools.partial(correlator_kernel, packed), name='correl...]
where the time goes in v5:
time: 86.3 us; the launch traced here: 85 us
  Pallas kernels  84.1 us (97%)
    pallas_call x1, Pallas kernels, correlator(): pl.pallas_call(functools.partial(correlator_kernel, packed), name='correl...  75.8 us
    pallas_call x1, Pallas kernels, unpack(): pl.pallas_call(unpack_kernel, name='unpack', grid=(rows // 16,), out_shap...  6.7 us

profile of v5, /device:TPU:0, one launch (start us, length us, event | category | flops | bytes accessed | tf_op | source)
XLA Modules:
  0.0 85.0 jit_solution(3903526767656080146)
XLA Ops:
  0.0 1.7 %prepare.1 = (f32[1,1024]{1,0:T(1,128)S(1)}, s32[1]{0:T(128)}) custom-call(s32[1,512]{1,0:T(1,128)} %bitcast.8), custom_call_target="tpu_custom_call" | custom-call | tf_op jit(solution)/shard_map/prepare/pallas_call | solution.py:519
  2.3 82.7 %conditional.1 = (f32[64,2,16,1024]{3,2,1,0:T(8,128)}) conditional(s32[]{:T(128)} %bitcast.4, (s32[8]{0:T(128)}, s32[8]{0:T(128)}, f32[12,1024]{1,0:T(8,128)}, f32[1,1024]{1,0:T(1,128)S(1)}, bf16[2,8,535552]{2,1,0:T(8,128)(2,1)}) %tuple.11, (s32[8]{0:T(128)}, s32[8]{0:T(128)}, f32[12,1024]{1,0:T(8,128)}, f32[1,1024]{1,0:T(1,128)S(1)}, ...), branch_computations={%region_0.0_spmd, %region_1.0_spmd} | conditional | flops 131078 | bytes 267086 | solution.py:544
  2.5 0.0 copy-start
  2.5 75.8 %correlator_packed.1 = (bf16[16,64,640]{2,1,0:T(8,128)(2,1)}, f32[1,1024]{1,0:T(1,128)}) custom-call(s32[8]{0:T(128)} %get-tuple-element.37.start_ref, s32[8]{0:T(128)} %get-tuple-element.38.count_ref, f32[12,1024]{1,0:T(8,128)} %get-tuple-element.39.taps_ref, f32[1,1024]{1,0:T(1,128)S(1)} %get-tuple-element.40.stations_ref, ...), custom_call_target="tpu_custom_call" | custom-call | tf_op jit(solution)/shard_map/cond/branch_1_fun/correlator_packed/pallas_call | solution.py:375
  78.3 0.0 copy-done
  78.3 6.7 %unpack.1 = f32[64,2,16,1024]{3,2,1,0:T(8,128)} custom-call(s32[512]{0:T(512)S(1)} %copy-done, bf16[16,64,640]{2,1,0:T(8,128)(2,1)} %get-tuple-element.42.in_ref, f32[1,1024]{1,0:T(1,128)} %get-tuple-element.43.place_ref, f32[1,1024]{1,0:T(1,128)S(1)} %get-tuple-element.40.stations_ref), custom_call_target="tpu_custom_call" | custom-call | tf_op jit(solution)/shard_map/cond/branch_1_fun/unpack/pallas_call | solution.py:485
Async XLA Ops:
  2.5 75.8 %copy-start = (s32[512]{0:T(512)S(1)}, s32[512]{0:T(512)}, u32[]{:S(2)}) copy-start(s32[512]{0:T(512)} %get-tuple-element.36.subarray_ref) | copy-start | bytes 6148 | tf_op jit(solution)/shard_map/cond
